TPU v7x, 32 devices: a whole 2x2x4 slice. The times are simulated.
32 devices in a mesh: req: 4 (over x, core), seq: 8 (over z, y).
Axes of the slice: x: 2, y: 2, z: 4, core: 2. Of those that a mesh axis runs over, the one named last changes fastest.
Arguments:
- conv_input: bfloat16 [4, 4096, 5120], P('req', 'seq'), may hold values from -6 to 6
- gate_projected: bfloat16 [4, 4096, 4096], P('req', 'seq'), may hold values from -6 to 6
- step_raw: float32 [4, 4096, 64], P('req', 'seq'), may hold values from -1.5 to 6.5
- step_bias: float32 [64], replicated, may hold values from -16 to -3
- decay_log: float32 [64], replicated, may hold values from -0.35 to 0.35
- head_direct_gain: float32 [64], replicated, may hold values from 0.2 to 1
- conv_weight: float32 [4, 5120], replicated, may hold values from -3 to 3
- convolution_bias: float32 [5120], replicated, may hold values from -0.5 to 0.5
- norm_weight: float32 [4096], replicated, may hold values from 0.5 to 1.5
- lengths: int32 [4, 4], P('req'), may hold values from 1 to 2048, 4096 in all within a row
- out_weight: bfloat16 [4096, 4096], P(('req', 'seq')), may hold values from -0.1875 to 0.1875
- residual_last: bfloat16 [4, 4, 4096], replicated, may hold values from -6 to 6
- final_gain: float32 [4096], replicated, may hold values from 0.5 to 1.5
- vocab_weight: bfloat16 [131072, 4096], P(('req', 'seq')), may hold values from -0.25 to 0.25
Outputs:
- y_gated: bfloat16 [4, 4096, 4096], P('req', 'seq')
- final_states: float32 [4, 4, 64, 64, 128], P('req', None, 'seq')
- last_hidden: bfloat16 [4, 4, 4096], P('req')
- max_logit: float32 [4, 4], P('req')
Inputs may be any that keep to these rules, and one draw needn't show every extreme that they name: The 4 lengths of a row sum to 4096.
All inputs are finite; a program needn't handle non-finite values.
Results may differ from a plain program's by a relative error of at most 0.0046.
Values may be sent and summed in bfloat16 or wider, within the bound.
No kernel may reach another device: no remote copies, remote signals or barrier semaphores. Data moves between devices by JAX's collectives and lax.ppermute only.
A program may use at most 256 MiB of HBM per device.

v0:
```python
import jax
import jax.numpy as jnp
from jax import lax
from jax.sharding import PartitionSpec as P

D = 4096
HEADS = 64
CHANNEL_WIDTH = 64
GROUPS = 4
STATE = 128
KERNEL = 4
BLOCK = 256
SEQS = 4


TINY_FLOOR = 1e-05


def from_behind(block, axis, distance):
    devices = range(lax.axis_size(axis))
    route = [(i - distance, i) for i in devices if i - distance in devices]
    return lax.ppermute(block, axis, route)


def segment_of(places, lengths):
    bounds = jnp.cumsum(lengths)[:-1]
    return jnp.sum((places[:, None] >= bounds[None, :]).astype(jnp.int32), axis=1)


def convolve(padded, padded_seg, conv_weight, convolution_bias, count):
    target = padded_seg[KERNEL - 1 :]
    total = jnp.zeros((count, padded.shape[1]), jnp.float32) + convolution_bias
    for kernel_tap in range(KERNEL):
        same_seg = (padded_seg[kernel_tap : kernel_tap + count] == target).astype(jnp.float32)
        total = (
            total
            + conv_weight[kernel_tap]
            * padded[kernel_tap : kernel_tap + count].astype(jnp.float32)
            * same_seg[:, None]
        )
    return jax.nn.silu(total)


def block_parts(
    feature_matrix,
    state_inputs,
    input_map,
    state_map,
    output_map,
    step_size,
    decays,
    segment,
    before,
):
    length = feature_matrix.shape[0]
    per_group = HEADS // GROUPS
    cum_decay = jnp.cumsum(decays, axis=0)
    places = jnp.arange(length)
    allowed = (places[:, None] >= places[None, :]) & (segment[:, None] == segment[None, :])
    spread = cum_decay.T[:, :, None] - cum_decay.T[:, None, :]
    weights = jnp.exp(jnp.where(allowed[None], spread, -jnp.inf)) * step_size.T[:, None, :]
    scores = jnp.einsum("tgn,sgn->gts", output_map, input_map, preferred_element_type=jnp.float32)
    mixing = (weights.reshape(GROUPS, per_group, length, length) * scores[:, None]).astype(
        jnp.bfloat16
    )
    grouped = feature_matrix.reshape(length, GROUPS, per_group, CHANNEL_WIDTH)
    y_intra = jnp.einsum(
        "gjts,sgjp->tgjp", mixing, grouped, preferred_element_type=jnp.float32
    ).reshape(length, HEADS, CHANNEL_WIDTH)
    tail_seg = (segment == segment[length - 1]).astype(jnp.float32)
    tail_weight = (
        jnp.exp(cum_decay[length - 1][None, :] - cum_decay) * step_size * tail_seg[:, None]
    )
    scaled = state_inputs * tail_weight[:, :, None]
    state = jnp.einsum(
        "sgjp,sgn->gjpn",
        scaled.reshape(length, GROUPS, per_group, CHANNEL_WIDTH),
        state_map,
        precision=lax.Precision.HIGHEST,
    ).reshape(HEADS, CHANNEL_WIDTH, STATE)
    within_tile = (segment == before).astype(jnp.float32)
    lead = jnp.exp(cum_decay) * within_tile[:, None]
    carry = jnp.exp(cum_decay[length - 1]) * within_tile[length - 1]
    return (y_intra, lead, state, carry)


def block_output(y_intra, lead, entering, output_map, feature_matrix, head_direct_gain):
    length = feature_matrix.shape[0]
    per_group = HEADS // GROUPS
    inter = jnp.einsum(
        "tgn,gjpn->tgjp",
        output_map.astype(jnp.float32),
        entering.reshape(GROUPS, per_group, CHANNEL_WIDTH, STATE),
        precision=lax.Precision.HIGHEST,
    ).reshape(length, HEADS, CHANNEL_WIDTH)
    return (
        y_intra
        + lead[:, :, None] * inter
        + head_direct_gain[None, :, None] * feature_matrix.astype(jnp.float32)
    )


def gate_norm(values, gate, norm_weight):
    length = values.shape[0]
    flat = values.reshape(length, -1) * jax.nn.silu(gate.astype(jnp.float32))
    grouped = flat.reshape(length, GROUPS, -1)
    scale = lax.rsqrt(jnp.mean(grouped * grouped, axis=-1, keepdims=True) + TINY_FLOOR)
    return ((grouped * scale).reshape(length, -1) * norm_weight).astype(jnp.bfloat16)


def state_at(state_inputs, state_map, step_size, decays, segment, before, within, entering):
    length = state_inputs.shape[0]
    per_group = HEADS // GROUPS
    cum_decay = jnp.cumsum(decays, axis=0)
    places = jnp.arange(length)
    allowed = (segment == segment[within]) & (places <= within)
    tail_weight = (
        jnp.exp(jnp.where(allowed[:, None], cum_decay[within][None, :] - cum_decay, -jnp.inf))
        * step_size
    )
    scaled = state_inputs * tail_weight[:, :, None]
    state = jnp.einsum(
        "sgjp,sgn->gjpn",
        scaled.reshape(length, GROUPS, per_group, CHANNEL_WIDTH),
        state_map,
        precision=lax.Precision.HIGHEST,
    ).reshape(HEADS, CHANNEL_WIDTH, STATE)
    lead = jnp.exp(cum_decay[within]) * (segment[within] == before).astype(jnp.float32)
    return lead[:, None, None] * entering + state


def body(
    conv_input,
    gate_projected,
    step_raw,
    step_bias,
    decay_log,
    head_direct_gain,
    conv_weight,
    convolution_bias,
    norm_weight,
    lengths,
    out_weight,
    residual_last,
    final_gain,
    vocab_weight,
):
    local_len = conv_input.shape[1]
    inner = HEADS * CHANNEL_WIDTH
    split_at = inner + GROUPS * STATE
    count = local_len // BLOCK
    seq_count = lax.axis_size("seq")
    seq_place = lax.axis_index("seq")
    req_place = lax.axis_index("req")
    first = seq_place * local_len
    length_row = lengths[0]
    own_rows = conv_input[0]
    edge = from_behind(own_rows[local_len - (KERNEL - 1) :], "seq", 1)
    padded = jnp.concatenate([edge, own_rows], axis=0)
    padded_places = first - (KERNEL - 1) + jnp.arange(local_len + KERNEL - 1, dtype=jnp.int32)
    padded_seg = segment_of(padded_places, length_row)
    segment = padded_seg[KERNEL - 1 :]
    mixed_full = convolve(padded, padded_seg, conv_weight, convolution_bias, local_len)
    mixed = mixed_full.astype(jnp.bfloat16)
    feature_matrix = mixed[:, :inner].reshape(local_len, HEADS, CHANNEL_WIDTH)
    input_map = mixed[:, inner:split_at].reshape(local_len, GROUPS, STATE)
    output_map = mixed[:, split_at:].reshape(local_len, GROUPS, STATE)
    state_inputs = mixed_full[:, :inner].reshape(local_len, HEADS, CHANNEL_WIDTH)
    state_map = mixed_full[:, inner:split_at].reshape(local_len, GROUPS, STATE)
    step_size = jax.nn.softplus(step_raw[0] + step_bias)
    decays = -jnp.exp(decay_log) * step_size
    befores = segment_of(first - 1 + BLOCK * jnp.arange(count, dtype=jnp.int32), length_row)
    block_inputs = feature_matrix.reshape(count, BLOCK, HEADS, CHANNEL_WIDTH)
    block_out_map = output_map.reshape(count, BLOCK, GROUPS, STATE)

    def local_pass(block):
        (
            part_inputs,
            part_state_inputs,
            part_in_map,
            part_state_map,
            part_out_map,
            part_step,
            part_decay,
            prompt_stretch,
            before,
        ) = block
        return block_parts(
            part_inputs,
            part_state_inputs,
            part_in_map,
            part_state_map,
            part_out_map,
            part_step,
            part_decay,
            prompt_stretch,
            before,
        )

    y_intra, leads, states, carries = lax.map(
        local_pass,
        (
            block_inputs,
            state_inputs.reshape(count, BLOCK, HEADS, CHANNEL_WIDTH),
            input_map.reshape(count, BLOCK, GROUPS, STATE),
            state_map.reshape(count, BLOCK, GROUPS, STATE),
            block_out_map,
            step_size.reshape(count, BLOCK, HEADS),
            decays.reshape(count, BLOCK, HEADS),
            segment.reshape(count, BLOCK),
            befores,
        ),
    )

    def fold(summary, block):
        carry, state = block
        return ((summary[0] * carry, carry[:, None, None] * summary[1] + state), None)

    (span_carry, span_state), _ = lax.scan(
        fold,
        (jnp.ones((HEADS,), jnp.float32), jnp.zeros((HEADS, CHANNEL_WIDTH, STATE), jnp.float32)),
        (carries, states),
    )

    def relay(turn, incoming):
        return from_behind(span_carry[:, None, None] * incoming + span_state, "seq", 1)

    entry_state = lax.fori_loop(0, seq_count - 1, relay, jnp.zeros_like(span_state))

    def enter(incoming, block):
        carry, state = block
        return (carry[:, None, None] * incoming + state, incoming)

    _, entering = lax.scan(enter, entry_state, (carries, states))

    def finish(block):
        part_intra, part_lead, part_enter, part_out_map, part_inputs, section_gate = block
        values = block_output(
            part_intra, part_lead, part_enter, part_out_map, part_inputs, head_direct_gain
        )
        return gate_norm(values, section_gate, norm_weight)

    gated = lax.map(
        finish,
        (
            y_intra,
            leads,
            entering,
            block_out_map,
            block_inputs,
            gate_projected[0].reshape(count, BLOCK, inner),
        ),
    ).reshape(local_len, inner)
    ends = jnp.cumsum(length_row) - 1
    finals = []
    lasts = []
    for request in range(SEQS):
        local_end = ends[request] - first
        owned = (local_end >= 0) & (local_end < local_len)
        spot = jnp.clip(local_end, 0, local_len - 1)
        index = spot // BLOCK
        start = index * BLOCK
        within = spot - start
        reached = state_at(
            lax.dynamic_slice_in_dim(state_inputs, start, BLOCK, 0),
            lax.dynamic_slice_in_dim(state_map, start, BLOCK, 0),
            lax.dynamic_slice_in_dim(step_size, start, BLOCK, 0),
            lax.dynamic_slice_in_dim(decays, start, BLOCK, 0),
            lax.dynamic_slice_in_dim(segment, start, BLOCK, 0),
            befores[index],
            within,
            entering[index],
        )
        finals.append(jnp.where(owned, reached, 0.0))
        lasts.append(jnp.where(owned, gated[spot].astype(jnp.float32), 0.0))
    final_terms = jnp.stack(finals)
    final_states = lax.psum_scatter(final_terms, "seq", scatter_dimension=1, tiled=True)[None]
    last_local = jnp.stack(lasts)
    rows_total = residual_last.shape[0]
    group_rows = lax.psum(last_local.astype(jnp.bfloat16), "seq")[None]
    all_rows = lax.all_gather(group_rows, "req", axis=0, tiled=True)
    share = out_weight.shape[0]
    flat_place = req_place * seq_count + seq_place
    columns = lax.dynamic_slice_in_dim(all_rows.reshape(-1, inner), flat_place * share, share, 1)
    partial_value = jnp.dot(columns, out_weight, preferred_element_type=jnp.float32)
    summed = lax.psum(partial_value, ("req", "seq"))
    hidden = residual_last.reshape(-1, D).astype(jnp.float32) + summed
    last_hidden = hidden.astype(jnp.bfloat16).reshape(rows_total, SEQS, D)
    own_hidden = lax.dynamic_slice_in_dim(last_hidden, req_place, 1, 0)
    scale = lax.rsqrt(jnp.mean(hidden * hidden, axis=-1, keepdims=True) + TINY_FLOOR)
    normed = (hidden * scale * final_gain).astype(jnp.bfloat16)
    logits = lax.dot_general(
        normed, vocab_weight, (((1,), (1,)), ((), ())), preferred_element_type=jnp.float32
    )
    local_top = jnp.max(logits, axis=1)
    top_all = lax.pmax(local_top, ("req", "seq"))
    max_logit = lax.dynamic_slice_in_dim(top_all.reshape(rows_total, SEQS), req_place, 1, 0)
    return (gated[None], final_states, own_hidden, max_logit)


def solution(mesh):
    return jax.shard_map(
        body,
        mesh=mesh,
        in_specs=(
            P("req", "seq", None),
            P("req", "seq", None),
            P("req", "seq", None),
            P(),
            P(),
            P(),
            P(),
            P(),
            P(),
            P("req", None),
            P(("req", "seq"), None),
            P(),
            P(),
            P(("req", "seq"), None),
        ),
        out_specs=(
            P("req", "seq", None),
            P("req", None, "seq", None, None),
            P("req", None, None),
            P("req", None),
        ),
        check_vma=False,
    )
```

profile of v0, /device:TPU:0, one launch (start us, length us, event | category | flops | bytes accessed | tf_op | source)
XLA Modules:
  0.0 937.5 jit_solution(7117656714561561972)
XLA Ops:
  9.1 4.9 collective-permute-start.1
  40.9 8.0 copy.137
  50.5 19.7 %fusion.69 = (bf16[512,5120]{0,1:T(8,128)(2,1)S(1)}, f32[512,5120]{0,1:T(8,128)S(1)}) fusion(bf16[512,5120]{0,1:T(8,128)(2,1)} %bitcast.396, f32[5120]{0:T(1024)S(1)} %bitcast.418, f32[512]{0:T(512)S(1)} %get-tuple-element.516, bf16[3,5120]{0,1:T(8,128)(2,1)} %copy.138, f32[5120]{0:T(1024)S(1)} %bitcast.419, f32[512]{0:T(512)S(1)} %get-tuple-element.517, ...), kind=kLoop, calls=%fused_computation.191 | loop fusion | flops 76021760 | bytes 21110784 | tf_op jit(solution)/shard_map/convert_element_type | solution.py:164
  73.6 4.2 slice.158
  82.8 10.6 %reshape_reshape.18 = f32[2,256,64,64]{1,0,3,2:T(2,128)} reshape(f32[512,4096]{0,1:T(8,128)} %slice.158) | data formatting | bytes 16777216 | tf_op jit(solution)/shard_map/reshape;reshape | solution.py:204
  93.3 6.9 reshape_reshape.15
  100.3 5.1 copy.142
  109.3 2.9 reshape.515
  114.7 90.1 %while.61 = (s32[]{:T(128)}, f32[2,256,64,64]{1,3,2,0:T(8,128)}, f32[2,256,64]{1,2,0:T(8,128)}, f32[2,64,64,128]{3,2,1,0:T(8,128)}, f32[2,64]{1,0:T(2,128)S(1)},...) while((s32[]{:T(128)}, f32[2,256,64,64]{1,3,2,0:T(8,128)}, ...), condition=%wide.region_6.7_spmd, body=%wide.region_3.6_spmd.sunk | while | flops 2239022336 | bytes 150750432 | solution.py:200
  121.3 9.8 %constant_dynamic-slice_fusion.24 = f32[1,256,64,64]{1,0,3,2:T(1,128)} fusion(f32[2,256,64,64]{1,0,3,2:T(2,128)} %get-tuple-element.839, s32[]{:T(128)} %get-tuple-element.809), kind=kLoop, calls=%fused_computation.67.clone.1 | loop fusion | bytes 8388612 | tf_op jit(solution)/shard_map/while/body/jit(dynamic_index_in_dim)/dynamic_slice | solution.py:200
  131.1 4.8 copy.265
  139.2 5.9 fusion.119
  151.0 4.5 fusion.117
  156.5 2.8 copy-done.7
  166.2 9.8 %constant_dynamic-slice_fusion.24 = f32[1,256,64,64]{1,0,3,2:T(1,128)} fusion(f32[2,256,64,64]{1,0,3,2:T(2,128)} %get-tuple-element.839, s32[]{:T(128)} %get-tuple-element.809), kind=kLoop, calls=%fused_computation.67.clone.1 | loop fusion | bytes 8388612 | tf_op jit(solution)/shard_map/while/body/jit(dynamic_index_in_dim)/dynamic_slice | solution.py:200
  175.9 4.8 copy.265
  184.0 5.9 fusion.119
  195.8 4.5 fusion.117
  204.8 4.0 while.65
  210.5 349.9 %while.62 = (s32[]{:T(128)}, f32[64,64,128]{2,1,0:T(8,128)S(1)}, f32[64]{0:T(128)S(1)}, f32[64,64,128]{2,1,0:T(8,128)}, s32[]{:T(128)}) while((s32[]{:T(128)}, f32[64,64,128]{2,1,0:T(8,128)S(1)}, f32[64]{0:T(128)S(1)}, f32[64,64,128]{2,1,0:T(8,128)}, s32[]{:T(128)}) %tuple.170), condition=%wide.region_10.11_spmd, body=%wide.region_9.10_spmd.sunk | while | flops 1048578 | bytes 14680421 | solution.py:228
  210.5 3.2 multiply_add_fusion.3
  213.6 3.6 collective-permute-start
  217.2 44.8 %collective-permute-done = f32[64,64,128]{2,1,0:T(8,128)S(1)} collective-permute-done((f32[64,64,128]{2,1,0:T(8,128)}, f32[64,64,128]{2,1,0:T(8,128)S(1)}, u32[]{:S(2)}, u32[]{:S(2)}) %collective-permute-start) | collective-permute-done | bytes 2097184 | tf_op jit(solution)/shard_map/while/body/eval_jaxpr/ppermute | solution.py:22
  262.0 3.2 multiply_add_fusion.3
  265.1 4.4 collective-permute-start
  269.5 43.9 %collective-permute-done = f32[64,64,128]{2,1,0:T(8,128)S(1)} collective-permute-done((f32[64,64,128]{2,1,0:T(8,128)}, f32[64,64,128]{2,1,0:T(8,128)S(1)}, u32[]{:S(2)}, u32[]{:S(2)}) %collective-permute-start) | collective-permute-done | bytes 2097184 | tf_op jit(solution)/shard_map/while/body/eval_jaxpr/ppermute | solution.py:22
  313.4 3.2 multiply_add_fusion.3
  316.5 4.5 collective-permute-start
  321.0 42.9 %collective-permute-done = f32[64,64,128]{2,1,0:T(8,128)S(1)} collective-permute-done((f32[64,64,128]{2,1,0:T(8,128)}, f32[64,64,128]{2,1,0:T(8,128)S(1)}, u32[]{:S(2)}, u32[]{:S(2)}) %collective-permute-start) | collective-permute-done | bytes 2097184 | tf_op jit(solution)/shard_map/while/body/eval_jaxpr/ppermute | solution.py:22
  363.9 3.2 multiply_add_fusion.3
  367.1 5.3 collective-permute-start
  372.4 42.0 %collective-permute-done = f32[64,64,128]{2,1,0:T(8,128)S(1)} collective-permute-done((f32[64,64,128]{2,1,0:T(8,128)}, f32[64,64,128]{2,1,0:T(8,128)S(1)}, u32[]{:S(2)}, u32[]{:S(2)}) %collective-permute-start) | collective-permute-done | bytes 2097184 | tf_op jit(solution)/shard_map/while/body/eval_jaxpr/ppermute | solution.py:22
  414.4 3.2 multiply_add_fusion.3
  417.6 5.3 collective-permute-start
  422.9 41.1 %collective-permute-done = f32[64,64,128]{2,1,0:T(8,128)S(1)} collective-permute-done((f32[64,64,128]{2,1,0:T(8,128)}, f32[64,64,128]{2,1,0:T(8,128)S(1)}, u32[]{:S(2)}, u32[]{:S(2)}) %collective-permute-start) | collective-permute-done | bytes 2097184 | tf_op jit(solution)/shard_map/while/body/eval_jaxpr/ppermute | solution.py:22
  464.0 3.2 multiply_add_fusion.3
  467.1 5.3 collective-permute-start
  472.4 40.2 %collective-permute-done = f32[64,64,128]{2,1,0:T(8,128)S(1)} collective-permute-done((f32[64,64,128]{2,1,0:T(8,128)}, f32[64,64,128]{2,1,0:T(8,128)S(1)}, u32[]{:S(2)}, u32[]{:S(2)}) %collective-permute-start) | collective-permute-done | bytes 2097184 | tf_op jit(solution)/shard_map/while/body/eval_jaxpr/ppermute | solution.py:22
  512.6 3.2 multiply_add_fusion.3
  515.8 5.3 collective-permute-start
  521.1 39.3 %collective-permute-done = f32[64,64,128]{2,1,0:T(8,128)S(1)} collective-permute-done((f32[64,64,128]{2,1,0:T(8,128)}, f32[64,64,128]{2,1,0:T(8,128)S(1)}, u32[]{:S(2)}, u32[]{:S(2)}) %collective-permute-start) | collective-permute-done | bytes 2097184 | tf_op jit(solution)/shard_map/while/body/eval_jaxpr/ppermute | solution.py:22
  562.9 6.8 while.63
  569.8 62.9 %while.64 = (s32[]{:T(128)}, bf16[2,256,4096]{2,1,0:T(8,128)(2,1)}, f32[2,256,64,64]{1,3,2,0:T(8,128)}, f32[2,256,64]{1,2,0:T(8,128)S(1)}, f32[2,64,64,128]{3,2,...) while((s32[]{:T(128)}, bf16[2,256,4096]{2,1,0:T(8,128)(2,1)}, ...), condition=%wide.region_16.17_spmd, body=%wide.region_13.16_spmd.sunk | while | flops 1638925312 | bytes 103515352 | solution.py:243
  571.6 3.8 fusion.123
  576.9 3.3 copy.268
  580.2 6.8 fusion.124
  589.7 7.1 fusion.125
  596.8 2.9 copy.269
  603.0 3.8 fusion.123
  608.3 3.3 copy.268
  611.6 6.8 fusion.124
  621.2 7.1 fusion.125
  628.3 2.9 copy.269
  633.8 38.7 %psum.14 = bf16[1,4,4096]{2,1,0:T(4,128)(2,1)S(1)} all-reduce(bf16[1,4,4096]{2,1,0:T(4,128)(2,1)S(1)} %maximum_bitcast_fusion), channel_id=1, replica_groups=mesh['req'=4,'seq'=8] {'seq'}, use_global_device_ids=true, to_apply=%region_26.27 | all-reduce | flops 16384 | bytes 65536 | tf_op jit(solution)/shard_map/psum | solution.py:280
  672.5 5.4 all_gather.3
  679.1 8.3 dynamic-slice_multiply_fusion.3
  687.4 3.9 fusion.46
  691.3 3.9 fusion.44
  695.2 3.9 fusion.42
  699.2 4.2 fusion.48
  707.7 8.0 copy.242
  716.6 151.5 %all-reduce.2.cloned.1.call-done = f32[16,4096]{1,0:T(8,128)} async-done(((f32[16,4096]{1,0:T(8,128)}), f32[16,4096]{1,0:T(8,128)}) %all-reduce.2.cloned.1.call-update) | async-done | bytes 262160 | tf_op jit(solution)/shard_map/psum | solution.py:286
  869.2 14.7 %convolution_reduce_fusion = f32[16]{0:T(128)S(1)} fusion(bf16[4096,4096]{1,0:T(8,128)(2,1)} %param.37, f32[16,4096]{1,0:T(8,128)S(1)} %get-tuple-element.474, f32[4096]{0:T(1024)S(1)} %copy-done.19, f32[16]{0:T(128)S(1)} %add_rsqrt_fusion.1), kind=kOutput, calls=%fused_computation.99 | convolution fusion | flops 537133056 | bytes 33833088 | tf_op jit(solution)/shard_map/dot_general | solution.py:292
  883.9 41.9 %pmax.7 = f32[4,4]{1,0:T(4,128)S(1)} all-reduce(f32[4,4]{1,0:T(4,128)S(1)} %reshape.504), channel_id=1, replica_groups=mesh['req'=4,'seq'=8] {'req','seq'}, use_global_device_ids=true, to_apply=%region_30.31 | all-reduce | flops 16 | bytes 128 | tf_op jit(solution)/shard_map/pmax | solution.py:296
  (257 shorter events, 114.9 us)
Async XLA Ops:
  8.0 670.0 %copy-start = (bf16[128,4096]{1,0:T(8,128)(2,1)S(1)}, bf16[128,4096]{1,0:T(8,128)(2,1)}, u32[]{:S(2)}) copy-start(bf16[128,4096]{1,0:T(8,128)(2,1)} %param.34) | copy-start | bytes 3145732
  8.0 860.1 %all-reduce.2.cloned.1.call-start = ((), (), s32[]{:S(2)}) async-start(), calls=%async_computation.1 | async-start | bytes 524288 | tf_op jit(solution)/shard_map/psum | solution.py:286
  9.1 39.9 %collective-permute-start.1 = (bf16[3,5120]{1,0:T(4,128)(2,1)S(1)}, bf16[3,5120]{1,0:T(4,128)(2,1)S(1)}, u32[]{:S(2)}, u32[]{:S(2)}) collective-permute-start(bf16[3,5120]{1,0:T(4,128)(2,1)S(1)} %slice_bitcast_fusion), channel_id=1, source_target_pairs={{0,1},{1,2},{2,3},{3,4},{4,5},{5,6},{6,7},{8,9},{9,10},{10,11},{11... | collective-permute-start | bytes 92168 | tf_op jit(solution)/shard_map/ppermute | solution.py:22
  40.9 9.7 %copy-start.21 = (f32[5120]{0:T(1024)S(1)}, f32[5120]{0:T(1024)}, u32[]{:S(2)}) copy-start(f32[5120]{0:T(1024)} %param.31) | copy-start | bytes 61444
  131.1 4.8 copy-start.11
  139.2 5.9 copy-start.3
  145.4 1.9 copy-start.4
  149.0 6.4 slice-start
  150.9 4.5 slice-start.1
  155.5 0.9 copy-start.12
  156.1 3.2 copy-start.7
  159.3 0.7 copy-start.13
  175.9 4.8 copy-start.11
  184.0 5.9 copy-start.3
  190.2 1.9 copy-start.4
  193.9 6.4 slice-start
  195.8 4.5 slice-start.1
  200.3 0.9 copy-start.12
  200.9 3.2 copy-start.7
  204.1 0.7 copy-start.13
  208.8 1.4 copy-start.2
  213.6 48.3 %collective-permute-start = (f32[64,64,128]{2,1,0:T(8,128)}, f32[64,64,128]{2,1,0:T(8,128)S(1)}, u32[]{:S(2)}, u32[]{:S(2)}) collective-permute-start(f32[64,64,128]{2,1,0:T(8,128)} %multiply_add_fusion.3), channel_id=1, source_target_pairs={{0,1},{1,2},{2,3},{3,4},{4,5},{5,6},{6,7},{8,9},{9,10},{10,11},{11... | collective-permute-start | bytes 6291464 | tf_op jit(solution)/shard_map/while/body/eval_jaxpr/ppermute | solution.py:22
  265.1 48.3 %collective-permute-start = (f32[64,64,128]{2,1,0:T(8,128)}, f32[64,64,128]{2,1,0:T(8,128)S(1)}, u32[]{:S(2)}, u32[]{:S(2)}) collective-permute-start(f32[64,64,128]{2,1,0:T(8,128)} %multiply_add_fusion.3), channel_id=1, source_target_pairs={{0,1},{1,2},{2,3},{3,4},{4,5},{5,6},{6,7},{8,9},{9,10},{10,11},{11... | collective-permute-start | bytes 6291464 | tf_op jit(solution)/shard_map/while/body/eval_jaxpr/ppermute | solution.py:22
  316.5 47.4 %collective-permute-start = (f32[64,64,128]{2,1,0:T(8,128)}, f32[64,64,128]{2,1,0:T(8,128)S(1)}, u32[]{:S(2)}, u32[]{:S(2)}) collective-permute-start(f32[64,64,128]{2,1,0:T(8,128)} %multiply_add_fusion.3), channel_id=1, source_target_pairs={{0,1},{1,2},{2,3},{3,4},{4,5},{5,6},{6,7},{8,9},{9,10},{10,11},{11... | collective-permute-start | bytes 6291464 | tf_op jit(solution)/shard_map/while/body/eval_jaxpr/ppermute | solution.py:22
  367.1 47.3 %collective-permute-start = (f32[64,64,128]{2,1,0:T(8,128)}, f32[64,64,128]{2,1,0:T(8,128)S(1)}, u32[]{:S(2)}, u32[]{:S(2)}) collective-permute-start(f32[64,64,128]{2,1,0:T(8,128)} %multiply_add_fusion.3), channel_id=1, source_target_pairs={{0,1},{1,2},{2,3},{3,4},{4,5},{5,6},{6,7},{8,9},{9,10},{10,11},{11... | collective-permute-start | bytes 6291464 | tf_op jit(solution)/shard_map/while/body/eval_jaxpr/ppermute | solution.py:22
  417.6 46.4 %collective-permute-start = (f32[64,64,128]{2,1,0:T(8,128)}, f32[64,64,128]{2,1,0:T(8,128)S(1)}, u32[]{:S(2)}, u32[]{:S(2)}) collective-permute-start(f32[64,64,128]{2,1,0:T(8,128)} %multiply_add_fusion.3), channel_id=1, source_target_pairs={{0,1},{1,2},{2,3},{3,4},{4,5},{5,6},{6,7},{8,9},{9,10},{10,11},{11... | collective-permute-start | bytes 6291464 | tf_op jit(solution)/shard_map/while/body/eval_jaxpr/ppermute | solution.py:22
  467.1 45.5 %collective-permute-start = (f32[64,64,128]{2,1,0:T(8,128)}, f32[64,64,128]{2,1,0:T(8,128)S(1)}, u32[]{:S(2)}, u32[]{:S(2)}) collective-permute-start(f32[64,64,128]{2,1,0:T(8,128)} %multiply_add_fusion.3), channel_id=1, source_target_pairs={{0,1},{1,2},{2,3},{3,4},{4,5},{5,6},{6,7},{8,9},{9,10},{10,11},{11... | collective-permute-start | bytes 6291464 | tf_op jit(solution)/shard_map/while/body/eval_jaxpr/ppermute | solution.py:22
  515.8 44.6 %collective-permute-start = (f32[64,64,128]{2,1,0:T(8,128)}, f32[64,64,128]{2,1,0:T(8,128)S(1)}, u32[]{:S(2)}, u32[]{:S(2)}) collective-permute-start(f32[64,64,128]{2,1,0:T(8,128)} %multiply_add_fusion.3), channel_id=1, source_target_pairs={{0,1},{1,2},{2,3},{3,4},{4,5},{5,6},{6,7},{8,9},{9,10},{10,11},{11... | collective-permute-start | bytes 6291464 | tf_op jit(solution)/shard_map/while/body/eval_jaxpr/ppermute | solution.py:22
  560.3 9.4 copy-start.14
  562.9 6.8 copy-start.15
  562.9 6.8 copy-start.20
  562.9 3.0 copy-start.5
  566.3 2.9 copy-start.5
  569.7 109.3 %copy-start.16 = (f32[256,64]{0,1:T(8,128)S(1)}, f32[256,64]{0,1:T(8,128)}, u32[]{:S(2)}) copy-start(f32[256,64]{0,1:T(8,128)} %get-tuple-element.503) | copy-start | bytes 196612
  569.7 109.3 %copy-start.17 = (f32[256,64]{0,1:T(8,128)S(1)}, f32[256,64]{0,1:T(8,128)}, u32[]{:S(2)}) copy-start(f32[256,64]{0,1:T(8,128)} %get-tuple-element.504) | copy-start | bytes 196612
  569.8 1.8 copy-start.9
  571.6 3.8 copy-start.8
  580.2 6.9 copy-start.1
  601.2 1.8 copy-start.9
  603.0 3.8 copy-start.8
  611.6 6.9 copy-start.1
  679.0 248.1 %reduce-scatter.5.cloned.1.call-start = ((), (), s32[]{:S(2)}) async-start(), calls=%async_computation.2 | async-start | bytes 9437184
  679.1 8.3 copy-start.10
  699.2 4.2 copy-start.6
  699.2 4.2 copy-start.22
  699.2 4.2 copy-start.23
  699.2 4.2 copy-start.24
  699.2 4.2 copy-start.25
  715.6 0.9 copy-start.18
  715.6 153.5 %copy-start.19 = (f32[4096]{0:T(1024)S(1)}, f32[4096]{0:T(1024)}, u32[]{:S(2)}) copy-start(f32[4096]{0:T(1024)} %param.36) | copy-start | bytes 49156
Sparse Core Ops, SparseCore 0:
  679.1 188.9 all-reduce.1
Sparse Core Ops, SparseCore 1:
  715.8 145.7 reduce-scatter.4
where the time goes:
time: 946 us; the launch traced here: 937 us
  waiting for transfers between devices  446 us (47%)
  local copies, waits for them, and re-layouts  167 us (18%)
  other arithmetic  112 us (12%)
  blocking collectives  86.1 us (9%)
  matrix products  62.7 us (7%)
  starting transfers between devices  38.6 us (4%)
  between operations  24.3 us (3%)
    ppermute x8, waiting for transfers between devices, from_behind(): return lax.ppermute(block, axis, route)  294 us
    psum x1, waiting for transfers between devices, body(): summed = lax.psum(partial_value, ('req', 'seq'))  152 us
    dynamic_slice x18, local copies, waits for them, and re-layouts, body(): lax.map(local_pass, (block_inputs, state_inputs.reshape(count, BLOCK, HEA...  42.9 us
    pmax x1, blocking collectives, body(): top_all = lax.pmax(local_top, ('req', 'seq'))  41.9 us
    psum x1, blocking collectives, body(): group_rows = lax.psum(last_local.astype(jnp.bfloat16), 'seq')[None]  38.7 us
    ppermute x8, starting transfers between devices, from_behind(): return lax.ppermute(block, axis, route)  38.5 us
    unnamed x38, local copies, waits for them, and re-layouts  22.4 us
    add x7, other arithmetic, relay(): span_carry[:, None, None] * incoming + span_state  22.1 us
  transfers between devices with their start and end apart: 10, of which 8 were waited for; matrix products, arithmetic and copies ran while one was open for 9% of the time, Pallas kernels for 0%

commit v1 on v0

v1 whole, which is shorter than its diff:
```python
import functools
import math

import jax
import jax.numpy as jnp
from jax import lax
from jax.experimental import pallas as pl
from jax.experimental.pallas import tpu as pltpu
from jax.sharding import PartitionSpec as P

D = 4096
HEADS = 64
WIDTH = 64
GROUPS = 4
STATE = 128
KERNEL = 4
SEQS = 4
INNER = HEADS * WIDTH
PER = HEADS // GROUPS
GW = INNER // GROUPS
Q = 128
EXTRA = 16
TINY_FLOOR = 1e-05
LOG2E = 1.0 / math.log(2.0)
BF = jnp.bfloat16
F32 = jnp.float32
HI = lax.Precision.HIGHEST
VM = 56 * 1024 * 1024


def params():
    return pltpu.CompilerParams(vmem_limit_bytes=VM)


def dot(a, b):
    return jnp.dot(a, b, preferred_element_type=F32)


def halves(x):
    hi = x.astype(BF)
    return hi, (x - hi.astype(F32)).astype(BF)


def spread(first_head, width):
    head = lax.broadcasted_iota(jnp.int32, (2 * HEADS, width), 0) % HEADS
    channel = lax.broadcasted_iota(jnp.int32, (2 * HEADS, width), 1)
    return (head == first_head + channel // WIDTH).astype(F32).astype(BF)


def silu(x):
    return x / (1.0 + jnp.exp(-x))


def segment(place, ends):
    return sum([(place >= ends[k]).astype(jnp.int32) for k in range(SEQS - 1)])


def prep_kernel(sc, dt_ref, log_ref, gain_ref, a_ref, b_ref, wst_ref, leadj_ref, lead0_ref, small_ref, cum, lj, l0, rows):
    T = dt_ref.shape[0]
    ends = [sc[k] for k in range(SEQS)]
    dt = dt_ref[...]
    dec = -jnp.exp(log_ref[...]) * dt
    later = lax.broadcasted_iota(jnp.int32, (T, T), 0)
    earlier = lax.broadcasted_iota(jnp.int32, (T, T), 1)
    total = jnp.dot((later >= earlier).astype(F32), dec, precision=HI, preferred_element_type=F32)
    cum[...] = total
    a2 = total * LOG2E
    for g in range(GROUPS):
        a_ref[g] = a2[:, g * PER : (g + 1) * PER]
    b_ref[...] = (a2 - jnp.log(dt) * LOG2E).T
    place = lax.broadcasted_iota(jnp.int32, (T, HEADS), 0)
    seg = segment(place, ends)
    lead0 = jnp.where(seg == segment(-1, ends), jnp.exp(total), 0.0)
    l0[...] = lead0
    stops = [cum[pl.ds(jnp.clip(ends[r] - 1, 0, T - 1), 1), :] for r in range(SEQS)]
    for j in range(T // Q):
        lo, hi = j * Q, (j + 1) * Q
        part = total[lo:hi]
        target = jnp.broadcast_to(total[hi - 1 : hi], (Q, HEADS))
        for r in range(SEQS - 1):
            target = jnp.where((seg[lo:hi] == r) & (ends[r] < hi), stops[r], target)
        weight = jnp.exp(target - part) * dt[lo:hi]
        wst_ref[lo:hi] = jnp.concatenate(halves(weight), axis=1)
        base = total[lo - 1 : lo] if j else 0.0
        lead = jnp.where(seg[lo:hi] == segment(lo - 1, ends), jnp.exp(part - base), 0.0)
        lj[lo:hi] = lead
        rows[j : j + 1] = lead[Q - 1 :]
    leadj_ref[...] = jnp.concatenate(halves(lj[...]), axis=1)
    lead0_ref[...] = jnp.concatenate(halves(lead0), axis=1)
    n = T // Q
    for r in range(SEQS):
        stop = ends[r] - 1
        owned = ((stop >= 0) & (stop < T)).astype(F32)
        at = pl.ds(jnp.clip(stop, 0, T - 1), 1)
        rows[n + r : n + r + 1] = lj[at, :] * owned
        rows[n + SEQS + r : n + SEQS + r + 1] = l0[at, :] * owned
    rows[n + 2 * SEQS : n + 2 * SEQS + 1] = lead0[T - 1 :]
    rows[n + 2 * SEQS + 1 : n + 2 * SEQS + 2] = gain_ref[...]
    small_ref[...] = jnp.concatenate(halves(rows[...]), axis=1)


def prep(scalars, dt, decay_log, gain):
    T = dt.shape[0]
    nrows = -(-(T // Q + 2 * SEQS + 2) // 16) * 16
    sds = jax.ShapeDtypeStruct
    return pl.pallas_call(
        prep_kernel,
        in_specs=[pl.BlockSpec(memory_space=pltpu.SMEM)] + [pl.BlockSpec(memory_space=pltpu.VMEM)] * 3,
        out_specs=[pl.BlockSpec(memory_space=pltpu.VMEM)] * 6,
        out_shape=[
            sds((GROUPS, T, PER), F32),
            sds((HEADS, T), F32),
            sds((T, 2 * HEADS), BF),
            sds((T, 2 * HEADS), BF),
            sds((T, 2 * HEADS), BF),
            sds((nrows, 2 * HEADS), BF),
        ],
        scratch_shapes=[
            pltpu.VMEM((T, HEADS), F32),
            pltpu.VMEM((T, HEADS), F32),
            pltpu.VMEM((T, HEADS), F32),
            pltpu.VMEM((nrows, HEADS), F32),
        ],
        compiler_params=params(),
        name="prep",
    )(scalars, dt, decay_log, gain)


def front_kernel(seqs, shard_w, sc, x_ref, b_ref, c_ref, hx, hb, hc, wx, wb, wc, bx, bb, bc, wst, small, gate,
                 xm, bm, cm, pay, eloc, slots, xs, act, ent, exs):
    T = x_ref.shape[0]
    n = T // Q
    g = pl.program_id(0)
    ends = [sc[k] for k in range(SEQS)]
    span = sc[SEQS]
    shards = GW // shard_w
    cuts = [slice(k * shard_w, (k + 1) * shard_w) for k in range(shards)]
    R = spread(g * PER, GW)
    wide = dot(small[...], R)
    packed = small[...].astype(F32)
    gain = wide[n + 2 * SEQS + 1 : n + 2 * SEQS + 2]
    pieces = [
        (x_ref, hx, wx, bx, xm, 0, GW),
        (b_ref, hb, wb, bb, bm, GW, STATE),
        (c_ref, hc, wc, bc, cm, GW + STATE, STATE),
    ]
    for src, halo, _, _, _, at, w in pieces:
        xs[0:8, at : at + w] = halo[...]
        xs[8:, at : at + w] = src[...].astype(F32)
    ent[...] = jnp.zeros_like(ent)
    slots[...] = jnp.zeros_like(slots)
    exs[...] = jnp.zeros_like(exs)
    for k in range(shards):
        exs[k, SEQS : 2 * SEQS, :] = gate[0:SEQS, cuts[k]]
        exs[k, 3 * SEQS : 3 * SEQS + 1, 0:128] = packed[n + 2 * SEQS : n + 2 * SEQS + 1]

    for j in range(n):
        lo = j * Q
        place = lo + lax.broadcasted_iota(jnp.int32, (Q, 128), 0)
        here = segment(place, ends)
        same = [(segment(place - 3 + k, ends) == here).astype(F32) for k in range(KERNEL - 1)]
        for src, _, w_ref, bias, out, at, w in pieces:
            for c in range(0, w, 128):
                col = slice(at + c, at + c + 128)
                acc = jnp.broadcast_to(bias[:, c : c + 128], (Q, 128))
                for k in range(KERNEL):
                    tap = w_ref[k : k + 1, c : c + 128] * xs[lo + 5 + k : lo + 5 + k + Q, col]
                    acc = acc + (tap * same[k] if k < KERNEL - 1 else tap)
                y = silu(acc)
                act[lo : lo + Q, col] = y
                out[lo : lo + Q, c : c + 128] = y.astype(BF)
        scaled = act[lo : lo + Q, :GW] * dot(wst[lo : lo + Q], R)
        xhi, xlo = halves(scaled)
        right = jnp.concatenate([xhi, xlo, xhi], axis=0)
        bt = act[lo : lo + Q, GW : GW + STATE].T
        lane_seg = segment(lo + lax.broadcasted_iota(jnp.int32, (STATE, Q), 1), ends)

        def gathered(which, bt=bt, lane_seg=lane_seg, right=right):
            bhi, blo = halves(jnp.where(lane_seg == which, bt, 0.0))
            return dot(jnp.concatenate([bhi, bhi, blo], axis=1), right)

        if j:
            eloc[j - 1] = ent[...].astype(BF)
        for r in range(SEQS):
            stop = ends[r] - 1

            @pl.when((stop >= lo) & (stop < lo + Q))
            def _(r=r, stop=stop, gathered=gathered):
                tail = wide[n + r : n + r + 1] * ent[...] + gathered(r)
                if r < SEQS - 1:
                    keep = stop < T - 1
                    if r != 1:
                        keep = keep & ((span < seqs // 2) if r == 0 else (span >= seqs // 2))

                    @pl.when(keep)
                    def _():
                        for k in range(shards):
                            slots[k, r % 2] = tail[:, cuts[k]].astype(BF)

                row = act[pl.ds(stop, 1), :].astype(BF)
                out_map = jnp.broadcast_to(row[:, GW + STATE :], (16, STATE))
                thi, tlo = halves(tail)
                value = (dot(out_map, thi) + dot(out_map, tlo))[0:1]
                value = value + gain * row[:, :GW].astype(F32)
                for k in range(shards):
                    exs[k, r : r + 1, :] = value[:, cuts[k]]
                    exs[k, 2 * SEQS + r : 2 * SEQS + r + 1, 0:128] = row[:, GW + STATE :].astype(F32)
                    exs[k, 2 * SEQS + r : 2 * SEQS + r + 1, 128:256] = packed[n + SEQS + r : n + SEQS + r + 1]

        ent[...] = wide[j : j + 1] * ent[...] + gathered(segment(lo + Q - 1, ends))
    for k in range(shards):
        pay[k, 0:STATE, :] = ent[:, cuts[k]].astype(BF)
        pay[k, STATE:, :] = exs[k].astype(BF)


def front(scalars, rows, halo, conv_weight, bias, wst, small, gate_rows, seqs):
    T = rows.shape[0]
    shard_w = INNER // seqs
    shards = GW // shard_w
    n = T // Q
    first_b, first_c = INNER // STATE, INNER // STATE + GROUPS
    sds = jax.ShapeDtypeStruct

    def three(height):
        return [
            pl.BlockSpec((height, GW), lambda g: (0, g)),
            pl.BlockSpec((height, STATE), lambda g: (0, first_b + g)),
            pl.BlockSpec((height, STATE), lambda g: (0, first_c + g)),
        ]

    whole = lambda a: pl.BlockSpec(a.shape, lambda g: (0, 0))
    return pl.pallas_call(
        functools.partial(front_kernel, seqs, shard_w),
        grid=(GROUPS,),
        in_specs=[pl.BlockSpec(memory_space=pltpu.SMEM)]
        + three(T)
        + three(8)
        + three(KERNEL)
        + three(1)
        + [whole(wst), whole(small), pl.BlockSpec((gate_rows.shape[0], GW), lambda g: (0, g))],
        out_specs=[
            pl.BlockSpec((T, GW), lambda g: (0, g)),
            pl.BlockSpec((T, STATE), lambda g: (0, g)),
            pl.BlockSpec((T, STATE), lambda g: (0, g)),
            pl.BlockSpec((shards, STATE + EXTRA, shard_w), lambda g: (g, 0, 0)),
            pl.BlockSpec((n - 1, STATE, GW), lambda g: (0, 0, g)),
            pl.BlockSpec((shards, 2, STATE, shard_w), lambda g: (g, 0, 0, 0)),
        ],
        out_shape=[
            sds((T, INNER), BF),
            sds((T, GROUPS * STATE), BF),
            sds((T, GROUPS * STATE), BF),
            sds((seqs, STATE + EXTRA, shard_w), BF),
            sds((n - 1, STATE, INNER), BF),
            sds((seqs, 2, STATE, shard_w), BF),
        ],
        scratch_shapes=[
            pltpu.VMEM((T + 8, GW + 2 * STATE), F32),
            pltpu.VMEM((T, GW + 2 * STATE), F32),
            pltpu.VMEM((STATE, GW), F32),
            pltpu.VMEM((shards, EXTRA, shard_w), F32),
        ],
        compiler_params=params(),
        name="front",
    )(scalars, rows, rows, rows, halo, halo, halo, conv_weight, conv_weight, conv_weight, bias, bias, bias, wst, small, gate_rows)


def local_kernel(gain_row, sc, x_ref, b_ref, c_ref, a_ref, bt_ref, lead, eloc, small, out):
    g, j = pl.program_id(0), pl.program_id(1)
    ends = [sc[k] for k in range(SEQS)]
    R = spread(g * PER, GW)
    wide = dot(small[...], R)
    gain = wide[gain_row : gain_row + 1]
    t = j * Q + lax.broadcasted_iota(jnp.int32, (Q, Q), 0)
    s = j * Q + lax.broadcasted_iota(jnp.int32, (Q, Q), 1)
    out_map = c_ref[...]
    scores = lax.dot_general(out_map, b_ref[...], (((1,), (1,)), ((), ())), preferred_element_type=F32)
    scores = jnp.where((s <= t) & (segment(t, ends) == segment(s, ends)), scores, 0.0)
    a, b = a_ref[0], bt_ref[...]
    low = (lax.broadcasted_iota(jnp.int32, (Q, 2 * WIDTH), 1) < WIDTH).astype(F32).astype(BF)
    high = 1 - low

    for p in range(PER // 2):
        col = slice(2 * p * WIDTH, 2 * (p + 1) * WIDTH)
        m = [
            (jnp.exp2(jnp.minimum(a[:, h : h + 1] - b[h : h + 1, :], 60.0)) * scores).astype(BF)
            for h in (2 * p, 2 * p + 1)
        ]
        x = x_ref[:, col]
        y = dot(jnp.concatenate(m, axis=1), jnp.concatenate([x * low, x * high], axis=0))
        out[:, col] = y + gain[:, col] * x.astype(F32)

    @pl.when(j > 0)
    def _():
        out[...] += dot(lead[...], R) * dot(out_map, eloc[0])


def local(scalars, xm, bm, cm, a2, b2, lead, eloc, small):
    T = xm.shape[0]
    return pl.pallas_call(
        functools.partial(local_kernel, T // Q + 2 * SEQS + 1),
        grid=(GROUPS, T // Q),
        in_specs=[
            pl.BlockSpec(memory_space=pltpu.SMEM),
            pl.BlockSpec((Q, GW), lambda g, j: (j, g)),
            pl.BlockSpec((Q, STATE), lambda g, j: (j, g)),
            pl.BlockSpec((Q, STATE), lambda g, j: (j, g)),
            pl.BlockSpec((1, Q, PER), lambda g, j: (g, j, 0)),
            pl.BlockSpec((PER, Q), lambda g, j: (g, j)),
            pl.BlockSpec((Q, 2 * HEADS), lambda g, j: (j, 0)),
            pl.BlockSpec((1, STATE, GW), lambda g, j: (jnp.maximum(j - 1, 0), 0, g)),
            pl.BlockSpec(small.shape, lambda g, j: (0, 0)),
        ],
        out_specs=pl.BlockSpec((Q, GW), lambda g, j: (j, g)),
        out_shape=jax.ShapeDtypeStruct((T, INNER), F32),
        compiler_params=params(),
        cost_estimate=pl.CostEstimate(flops=8 * 10**9, bytes_accessed=2 * 10**7, transcendentals=5 * 10**6),
        name="local",
    )(scalars, xm, bm, cm, a2, b2, lead, eloc, small)


def scan_kernel(sc, got, enter, base, value, ent):
    seqs, _, shard_w = got.shape
    R = spread(sc[2 * SEQS] * (shard_w // WIDTH), shard_w)
    ent[...] = jnp.zeros_like(ent)
    value[...] = jnp.zeros_like(value)
    for i in range(seqs):
        now = ent[...]
        enter[i] = now.astype(BF)
        state = got[i, 0:STATE].astype(F32)
        extra = got[i, STATE:]
        carry = dot(extra[:, 0:128], R)[3 * SEQS : 3 * SEQS + 1]
        for r in range(SEQS):

            @pl.when(sc[r] == i)
            def _(r=r, now=now, state=state, extra=extra):
                at = slice(2 * SEQS + r, 2 * SEQS + r + 1)
                lead = dot(extra[:, 128:256], R)[at]
                base[r] = lead * now + jnp.where(sc[SEQS + r] == 1, state, 0.0)
                hi, lo = halves(now)
                inter = (dot(extra[:, 0:128], hi) + dot(extra[:, 0:128], lo))[at]
                rows = extra.astype(F32)
                value[r : r + 1, :] = (rows[r : r + 1] + lead * inter) * silu(rows[SEQS + r : SEQS + r + 1])

        ent[...] = carry * now + state


def scan(scalars, got):
    seqs, _, shard_w = got.shape
    sds = jax.ShapeDtypeStruct
    return pl.pallas_call(
        scan_kernel,
        in_specs=[pl.BlockSpec(memory_space=pltpu.SMEM), pl.BlockSpec(memory_space=pltpu.VMEM)],
        out_specs=[pl.BlockSpec(memory_space=pltpu.VMEM)] * 3,
        out_shape=[
            sds((seqs, STATE, shard_w), BF),
            sds((SEQS, STATE, shard_w), F32),
            sds((8, shard_w), F32),
        ],
        scratch_shapes=[pltpu.VMEM((STATE, shard_w), F32)],
        compiler_params=params(),
        name="scan",
    )(scalars, got)


def finals_kernel(sc, base, tail, out):
    r = pl.program_id(0)
    use = (r < SEQS - 1) & (sc[SEQS + r] == 0)
    out[0] = (base[0] + jnp.where(use, tail[0, 0].astype(F32), 0.0)).T


def finals(scalars, base, tails):
    _, _, shard_w = base.shape
    return pl.pallas_call(
        finals_kernel,
        grid_spec=pltpu.PrefetchScalarGridSpec(
            num_scalar_prefetch=1,
            grid=(SEQS,),
            in_specs=[
                pl.BlockSpec((1, STATE, shard_w), lambda r, sc: (r, 0, 0)),
                pl.BlockSpec((1, 1, STATE, shard_w), lambda r, sc: (sc[r], r % 2, 0, 0)),
            ],
            out_specs=pl.BlockSpec((1, shard_w, STATE), lambda r, sc: (r, 0, 0)),
        ),
        out_shape=jax.ShapeDtypeStruct((SEQS, shard_w, STATE), F32),
        compiler_params=params(),
        name="finals",
    )(scalars, base, tails)


def finish_kernel(y_ref, gate, c_ref, e_ref, lead, norm, out):
    R = spread(pl.program_id(0) * PER, GW)
    entering = jnp.concatenate([e_ref[k] for k in range(e_ref.shape[0])], axis=1)
    y = y_ref[...] + dot(lead[...], R) * dot(c_ref[...], entering)
    v = y * silu(gate[...].astype(F32))
    scale = lax.rsqrt(jnp.sum(v * v, axis=1, keepdims=True) * (1.0 / GW) + TINY_FLOOR)
    out[...] = (v * scale * norm[...]).astype(BF)


def finish(y_local, gate, cm, enter, lead, norm):
    T = y_local.shape[0]
    seqs, _, shard_w = enter.shape
    tile = 256
    return pl.pallas_call(
        finish_kernel,
        grid=(GROUPS, T // tile),
        in_specs=[
            pl.BlockSpec((tile, GW), lambda g, i: (i, g)),
            pl.BlockSpec((tile, GW), lambda g, i: (i, g)),
            pl.BlockSpec((tile, STATE), lambda g, i: (i, g)),
            pl.BlockSpec((GW // shard_w, STATE, shard_w), lambda g, i: (g, 0, 0)),
            pl.BlockSpec((tile, 2 * HEADS), lambda g, i: (i, 0)),
            pl.BlockSpec((1, GW), lambda g, i: (0, g)),
        ],
        out_specs=pl.BlockSpec((tile, GW), lambda g, i: (i, g)),
        out_shape=jax.ShapeDtypeStruct((T, INNER), BF),
        compiler_params=params(),
        cost_estimate=pl.CostEstimate(flops=2 * 10**9, bytes_accessed=2 * 10**7, transcendentals=4 * 10**6),
        name="finish",
    )(y_local, gate, cm, enter, lead, norm)


def exchange(x, axes):
    return lax.all_to_all(x, axes, 0, 0, tiled=True)


def body(
    conv_input,
    gate_projected,
    step_raw,
    step_bias,
    decay_log,
    head_direct_gain,
    conv_weight,
    convolution_bias,
    norm_weight,
    lengths,
    out_weight,
    residual_last,
    final_gain,
    vocab_weight,
):
    every = ("req", "seq")
    T = conv_input.shape[1]
    seqs, reqs = lax.axis_size("seq"), lax.axis_size("req")
    seq_place, req_place = lax.axis_index("seq"), lax.axis_index("req")
    devices = seqs * reqs
    flat = req_place * seqs + seq_place
    shard_w = INNER // seqs
    share = out_weight.shape[0]
    rows_total = reqs * SEQS
    rows = conv_input[0]

    edge = lax.ppermute(rows[T - (KERNEL - 1) :], "seq", [(i, i + 1) for i in range(seqs - 1)])
    halo = jnp.pad(edge.astype(F32), ((8 - (KERNEL - 1), 0), (0, 0)))
    ends = jnp.cumsum(lengths[0]).astype(jnp.int32)
    local_ends = ends - seq_place * T
    scalars = jnp.concatenate([local_ends, seq_place[None].astype(jnp.int32)])
    last = ends - 1
    owner = last // T
    at_end = (ends % T == 0).astype(jnp.int32)
    owners = jnp.concatenate([owner, at_end, seq_place[None].astype(jnp.int32)])

    dt = jax.nn.softplus(step_raw[0] + step_bias)
    stop = local_ends - 1
    owned = (stop >= 0) & (stop < T)
    gate_rows = gate_projected[0][jnp.clip(stop, 0, T - 1)].astype(F32)
    gate_rows = jnp.pad(jnp.where(owned[:, None], gate_rows, 0.0), ((0, 8 - SEQS), (0, 0)))

    a2, b2, wst, leadj, lead0, small = prep(scalars, dt, decay_log[None], head_direct_gain[None])
    xm, bm, cm, pay, eloc, slots = front(
        scalars, rows, halo, conv_weight, convolution_bias[None], wst, small, gate_rows, seqs
    )
    got = exchange(pay, "seq")
    y_local = local(scalars, xm, bm, cm, a2, b2, leadj, eloc, small)
    enter, base, value = scan(owners, got)
    entering = exchange(enter, "seq")

    parts = shard_w // share
    mine = value[:SEQS].reshape(SEQS, parts, share).transpose(1, 0, 2)
    mail = lax.dynamic_update_slice(jnp.zeros((devices, SEQS, share), F32), mine, (seq_place * parts, 0, 0))
    mail = exchange(mail, every).reshape(reqs, seqs, SEQS, share)
    v = lax.dynamic_index_in_dim(mail, flat * share // shard_w, 1, keepdims=False).reshape(rows_total, share)
    squares = jnp.sum(v * v, axis=1)
    u = (v * lax.dynamic_slice_in_dim(norm_weight, flat * share, share)).astype(BF)
    partial = jnp.dot(u, out_weight, preferred_element_type=F32)
    chunk = D // devices
    mail = partial.reshape(rows_total, devices, chunk).transpose(1, 0, 2)
    line = jnp.pad(squares, (0, chunk - rows_total))
    mail = jnp.concatenate([mail, jnp.broadcast_to(line, (devices, 8, chunk))], axis=1)
    mail = exchange(mail, every)
    sums = mail.reshape(GROUPS, devices // GROUPS, rows_total + 8, chunk).sum(axis=1)
    scale = lax.rsqrt(sums[:, rows_total, :rows_total] * (1.0 / GW) + TINY_FLOOR)
    own = jnp.sum(scale[:, :, None] * sums[:, :rows_total], axis=0)
    residual = residual_last.reshape(rows_total, D)
    own = own + lax.dynamic_slice_in_dim(residual, flat * chunk, chunk, 1).astype(F32)
    mail = exchange(jnp.broadcast_to(own, (devices, rows_total, chunk)), every)
    hidden = mail.transpose(1, 0, 2).reshape(rows_total, D)
    rms = lax.rsqrt(jnp.mean(hidden * hidden, axis=-1, keepdims=True) + TINY_FLOOR)
    normed = (hidden * rms * final_gain).astype(BF)
    last_hidden = lax.dynamic_slice_in_dim(hidden.reshape(reqs, SEQS, D), req_place, 1, 0).astype(BF)

    y_gated = finish(y_local, gate_projected[0], cm, entering, lead0, norm_weight[None])

    logits = lax.dot_general(normed, vocab_weight, (((1,), (1,)), ((), ())), preferred_element_type=F32)
    top = jnp.max(logits, axis=1).reshape(reqs, 1, SEQS)
    top = jnp.broadcast_to(top, (reqs, seqs, SEQS)).reshape(devices, SEQS)
    max_logit = jnp.max(exchange(top, every), axis=0, keepdims=True)

    tails = exchange(slots, "seq")
    final_states = finals(owners, base, tails).reshape(1, SEQS, HEADS // seqs, WIDTH, STATE)
    return (y_gated[None], final_states, last_hidden, max_logit)


def solution(mesh):
    return jax.shard_map(
        body,
        mesh=mesh,
        in_specs=(
            P("req", "seq", None),
            P("req", "seq", None),
            P("req", "seq", None),
            P(),
            P(),
            P(),
            P(),
            P(),
            P(),
            P("req", None),
            P(("req", "seq"), None),
            P(),
            P(),
            P(("req", "seq"), None),
        ),
        out_specs=(
            P("req", "seq", None),
            P("req", None, "seq", None, None),
            P("req", None, None),
            P("req", None),
        ),
        check_vma=False,
    )
```

time: 946 us -> 248 us (0.26)
  waiting for transfers between devices: 446 us -> 47.6 us
  local copies, waits for them, and re-layouts: 167 us -> 12.5 us
  other arithmetic: 112 us -> 6.06 us
  Pallas kernels: 0 us -> 68.3 us
  matrix products: 62.7 us -> 15.2 us
  between operations: 24.3 us -> 0.84 us
  starting transfers between devices: 38.6 us -> 22.4 us
  blocking collectives: 86.1 us -> 73.5 us
    ppermute x8 -> x1, waiting for transfers between devices: 294 us -> 0.01 us  [body(): lax.ppermute(rows[T - (KERNEL - 1):], 'seq', [(i, i + 1) for i in range(s...]
    psum x1 -> x0, waiting for transfers between devices: 152 us -> none  [body(): summed = lax.psum(partial_value, ('req', 'seq'))]
    all_to_all x0 -> x3, blocking collectives: none -> 73.5 us  [exchange(): return lax.all_to_all(x, axes, 0, 0, tiled=True)]
    pallas_call x0 -> x6, Pallas kernels: none -> 68.3 us  [the longest x1 25.3 us: front(): pl.pallas_call(functools.partial(front_kernel, seqs, shard_w), grid=(GROU...]
    dynamic_slice x28 -> x1, local copies, waits for them, and re-layouts: 58.4 us -> 0.77 us  [body(): lax.dynamic_slice_in_dim(norm_weight, flat * share, share)]
    dot_general x13 -> x1, matrix products: 48 us -> 0.37 us  [body(): partial = jnp.dot(u, out_weight, preferred_element_type=F32)]
    all_to_all x0 -> x4, waiting for transfers between devices: none -> 47.6 us  [exchange(): return lax.all_to_all(x, axes, 0, 0, tiled=True)]
    pmax x1 -> x0, blocking collectives: 41.9 us -> none  [body(): top_all = lax.pmax(local_top, ('req', 'seq'))]
  transfers between devices with their start and end apart: 10 -> 5, of which waited for: 8 -> 4; matrix products, arithmetic and copies ran while one was open for 9% -> 5% of each run, Pallas kernels for 0% -> 11%
where the time goes in v1:
time: 248 us; the launch traced here: 246 us
  blocking collectives  73.5 us (30%)
  Pallas kernels  68.3 us (28%)
  waiting for transfers between devices  47.6 us (19%)
  starting transfers between devices  22.4 us (9%)
  matrix products  15.2 us (6%)
  local copies, waits for them, and re-layouts  12.5 us (5%)
  other arithmetic  6.06 us (2%)
    all_to_all x3, blocking collectives, exchange(): return lax.all_to_all(x, axes, 0, 0, tiled=True)  73.5 us
    all_to_all x4, waiting for transfers between devices, exchange(): return lax.all_to_all(x, axes, 0, 0, tiled=True)  47.6 us
    pallas_call x1, Pallas kernels, front(): pl.pallas_call(functools.partial(front_kernel, seqs, shard_w), grid=(GROU...  25.3 us
    pallas_call x1, Pallas kernels, local(): pl.pallas_call(functools.partial(local_kernel, T // Q + 2 * SEQS + 1), gr...  18.8 us
    all_to_all x4, starting transfers between devices, exchange(): return lax.all_to_all(x, axes, 0, 0, tiled=True)  17.5 us
    dot_general x1, matrix products, body(): lax.dot_general(normed, vocab_weight, (((1,), (1,)), ((), ())), preferred...  14.8 us
    pallas_call x1, Pallas kernels, finish(): pl.pallas_call(finish_kernel, grid=(GROUPS, T // tile), in_specs=[pl.Bloc...  11.4 us
  transfers between devices with their start and end apart: 5, of which 4 were waited for; matrix products, arithmetic and copies ran while one was open for 5% of the time, Pallas kernels for 11%

profile of v1, /device:TPU:0, one launch (start us, length us, event | category | flops | bytes accessed | tf_op | source)
XLA Modules:
  0.0 246.3 jit_solution(2332155295263037298)
XLA Ops:
  0.6 0.9 slice_bitcast_fusion
  1.5 4.9 %collective-permute-start = (bf16[3,5120]{1,0:T(4,128)(2,1)S(1)}, bf16[3,5120]{1,0:T(4,128)(2,1)S(1)}, u32[]{:S(2)}, u32[]{:S(2)}) collective-permute-start(bf16[3,5120]{1,0:T(4,128)(2,1)S(1)} %slice_bitcast_fusion), channel_id=1, source_target_pairs={{0,1},{1,2},{2,3},{3,4},{4,5},{5,6},{6,7},{8,9},{9,10},{10,11},{11... | collective-permute-start | bytes 92168 | tf_op jit(solution)/shard_map/ppermute | solution.py:454
  6.4 0.8 reduce-window.4
  7.3 1.0 copy.49
  8.3 1.5 compare_select_fusion.dt_ref
  9.9 3.3 %gather_fusion = bf16[4,4096]{1,0:T(4,128)(2,1)S(1)} fusion(bf16[512,4096]{1,0:T(8,128)(2,1)} %bitcast.61, s32[1024]{0:T(1024)S(1)} %pad_clamp_fusion), kind=kCustom, calls=%fused_computation | custom fusion | bytes 65552 | tf_op jit(solution)/shard_map/gather | solution.py:467
  13.2 0.1 convert_select_fusion
  13.3 0.6 pad_add_fusion.sc
  13.9 0.7 pad.16.gate
  14.6 3.5 %prep.1 = (f32[4,512,16]{2,1,0:T(8,128)}, f32[64,512]{1,0:T(8,128)}, bf16[512,128]{1,0:T(8,128)(2,1)}, bf16[512,128]{1,0:T(8,128)(2,1)}, bf16[512,128]{1,0:T(8,128)(2,1)}, /*index=5*/bf16[16,128]{1,0:T(8,128)(2,1)}) custom-call(s32[5]{0:T(128)} %pad_add_fusion.sc, f32[512,64]{1,0:T(8,128)} %compare_select_fusion.dt_ref, f32[1,64]{1,0:T(1,128)} %bitcast.76, ...), custom_call_target="tpu_custom_call" | custom-call | tf_op jit(solution)/shard_map/prep/pallas_call | solution.py:106
  18.0 0.0 collective-permute-done
  18.0 0.7 pad_convert_fusion.hx.hb.hc
  18.7 25.3 %front.1 = (bf16[512,4096]{1,0:T(8,128)(2,1)}, bf16[512,512]{1,0:T(8,128)(2,1)}, bf16[512,512]{1,0:T(8,128)(2,1)}, bf16[8,144,512]{2,1,0:T(8,128)(2,1)}, bf16[3,...) custom-call(s32[5]{0:T(128)} %pad_add_fusion.sc, bf16[512,5120]{1,0:T(8,128)(2,1)} %bitcast.58, ...), custom_call_target="tpu_custom_call" | custom-call | tf_op jit(solution)/shard_map/front/pallas_call | solution.py:232
  44.0 0.0 copy-start.3
  44.1 0.0 copy-start.4
  44.1 7.8 %all-to-all-start = ((bf16[8,144,512]{2,1,0:T(8,128)(2,1)}), bf16[8,144,512]{2,1,0:T(8,128)(2,1)S(1)}, u32[]{:S(2)}, u32[]{:S(2)}) async-start(bf16[8,144,512]{2,1,0:T(8,128)(2,1)} %get-tuple-element.28), calls=%async_computation | async-start | bytes 2359296 | tf_op jit(solution)/shard_map/all_to_all | solution.py:424
  51.9 0.6 pad_add_fusion.1.sc
  52.5 0.0 copy-start.5
  52.5 27.2 %all-to-all-done.got = bf16[8,144,512]{2,1,0:T(8,128)(2,1)S(1)} async-done(((bf16[8,144,512]{2,1,0:T(8,128)(2,1)}), bf16[8,144,512]{2,1,0:T(8,128)(2,1)S(1)}, u32[]{:S(2)}, u32[]{:S(2)}) %all-to-all-start) | async-done | bytes 1179680 | tf_op jit(solution)/shard_map/all_to_all | solution.py:424
  79.7 0.0 copy-start
  79.7 1.0 copy-done
  80.7 4.9 %scan.1 = (bf16[8,128,512]{2,1,0:T(8,128)(2,1)}, f32[4,128,512]{2,1,0:T(8,128)}, f32[8,512]{1,0:T(8,128)}) custom-call(s32[9]{0:T(128)} %pad_add_fusion.1.sc, bf16[8,144,512]{2,1,0:T(8,128)(2,1)} %copy-done), custom_call_target="tpu_custom_call" | custom-call | tf_op jit(solution)/shard_map/scan/pallas_call | solution.py:351
  85.7 0.6 broadcast_in_dim.65
  86.3 1.3 bitcast_dynamic-update-slice_fusion
  87.6 3.5 %all-to-all-start.3 = ((f32[32,4,128]{2,1,0:T(4,128)}), f32[32,4,128]{2,1,0:T(4,128)S(1)}, u32[]{:S(2)}, u32[]{:S(2)}) async-start(f32[32,4,128]{2,1,0:T(4,128)} %bitcast_dynamic-update-slice_fusion), calls=%async_computation.3 | async-start | bytes 131072 | tf_op jit(solution)/shard_map/all_to_all | solution.py:424
  91.1 0.0 copy-done.3
  91.1 0.7 copy.61
  91.8 0.8 dynamic_slice.14
  92.5 5.8 %all-to-all-done.3 = f32[32,4,128]{2,1,0:T(4,128)S(1)} async-done(((f32[32,4,128]{2,1,0:T(4,128)}), f32[32,4,128]{2,1,0:T(4,128)S(1)}, u32[]{:S(2)}, u32[]{:S(2)}) %all-to-all-start.3) | async-done | bytes 65568 | tf_op jit(solution)/shard_map/all_to_all | solution.py:424
  98.3 0.1 multiply_convert_fusion
  98.4 0.1 reduce_sum.39
  98.5 0.4 convolution_bitcast_fusion
  98.9 0.8 pad_maximum_fusion
  99.7 2.6 %all-to-all-start.4 = ((f32[32,24,128]{2,1,0:T(8,128)}), f32[32,24,128]{2,1,0:T(8,128)S(1)}, u32[]{:S(2)}, u32[]{:S(2)}) async-start(f32[32,24,128]{2,1,0:T(8,128)} %pad_maximum_fusion), calls=%async_computation.4 | async-start | bytes 786432 | tf_op jit(solution)/shard_map/all_to_all | solution.py:424
  102.3 0.0 copy-done.4
  102.4 13.5 %all-to-all-done.4 = f32[32,24,128]{2,1,0:T(8,128)S(1)} async-done(((f32[32,24,128]{2,1,0:T(8,128)}), f32[32,24,128]{2,1,0:T(8,128)S(1)}, u32[]{:S(2)}, u32[]{:S(2)}) %all-to-all-start.4) | async-done | bytes 393248 | tf_op jit(solution)/shard_map/all_to_all | solution.py:424
  115.9 0.1 fusion.5
  116.0 12.6 %all_to_all.39 = f32[32,16,128]{2,1,0:T(8,128)S(1)} all-to-all(f32[32,16,128]{2,1,0:T(8,128)S(1)} %broadcast_in_dim.67), channel_id=1, replica_groups=mesh['req'=4,'seq'=8] {'req','seq'}, dimensions={0} | all-to-all | bytes 524288 | tf_op jit(solution)/shard_map/all_to_all | solution.py:424
  128.6 0.1 multiply_reduce_fusion
  128.8 0.0 copy-done.5
  128.8 0.0 copy-start.2
  128.8 14.8 %convolution_reduce_fusion = f32[16]{0:T(128)S(1)} fusion(bf16[4096,4096]{1,0:T(8,128)(2,1)} %param.27, f32[4096]{0:T(1024)S(1)} %copy-done.5, f32[16]{0:T(128)S(1)} %add_rsqrt_fusion, f32[32,16,128]{2,1,0:T(8,128)S(1)} %all_to_all.39), kind=kOutput, calls=%fused_computation.2 | convolution fusion | flops 537133056 | bytes 33833088 | tf_op jit(solution)/shard_map/dot_general | solution.py:505
  143.6 0.1 broadcast_in_dim.68
  143.7 9.3 %all_to_all.40 = f32[32,1,4]{2,1,0:T(1,128)S(1)} all-to-all(f32[32,1,4]{2,1,0:T(1,128)S(1)} %bitcast.72), channel_id=1, replica_groups=mesh['req'=4,'seq'=8] {'req','seq'}, dimensions={0} | all-to-all | bytes 1024 | tf_op jit(solution)/shard_map/all_to_all | solution.py:424
  153.0 0.0 copy-done.2
  153.0 51.6 %all_to_all.41.tail = bf16[8,2,128,512]{3,2,1,0:T(8,128)(2,1)} all-to-all(bf16[8,2,128,512]{3,2,1,0:T(8,128)(2,1)S(1)} %copy-done.2), channel_id=1, replica_groups=mesh['req'=4,'seq'=8] {'seq'}, dimensions={0} | all-to-all | bytes 4194304 | tf_op jit(solution)/shard_map/all_to_all | solution.py:424
  204.6 3.6 %all-to-all-start.1 = ((bf16[8,128,512]{2,1,0:T(8,128)(2,1)}), bf16[8,128,512]{2,1,0:T(8,128)(2,1)S(1)}, u32[]{:S(2)}, u32[]{:S(2)}) async-start(bf16[8,128,512]{2,1,0:T(8,128)(2,1)} %get-tuple-element.29), calls=%async_computation.1 | async-start | bytes 2097152 | tf_op jit(solution)/shard_map/all_to_all | solution.py:424
  208.2 18.8 %local.1.y_ref = f32[512,4096]{1,0:T(8,128)} custom-call(s32[5]{0:T(128)} %pad_add_fusion.sc, bf16[512,4096]{1,0:T(8,128)(2,1)} %get-tuple-element.21.x_ref, bf16[512,512]{1,0:T(8,128)(2,1)} %get-tuple-element.22.b_ref, bf16[512,512]{1,0:T(8,128)(2,1)} %get-tuple-element.23.c_ref, f32[4,512,16]{2,1,0:T(8,128)} %get-tuple-element.24.a_ref, ...), custom_call_target="tpu_custom_call" | custom-call | flops 8000000000 | bytes 20000000 | tf_op jit(solution)/shard_map/local/pallas_call | solution.py:300
  227.0 0.1 copy.56
  227.2 0.6 dynamic-slice_convert_fusion
  227.8 0.6 reduce_max.19
  228.4 4.4 %finals.1 = f32[4,512,128]{2,1,0:T(8,128)} custom-call(s32[9]{0:T(128)} %pad_add_fusion.1.sc, f32[4,128,512]{2,1,0:T(8,128)} %get-tuple-element.31.base, bf16[8,2,128,512]{3,2,1,0:T(8,128)(2,1)} %all_to_all.41.tail), custom_call_target="tpu_custom_call" | custom-call | tf_op jit(solution)/shard_map/finals/pallas_call | solution.py:374
  232.7 1.1 all-to-all-done.1.e_ref
  233.9 0.0 copy-start.1
  233.9 1.1 copy-done.1
  234.9 11.4 %finish.1 = bf16[512,4096]{1,0:T(8,128)(2,1)} custom-call(f32[512,4096]{1,0:T(8,128)} %local.1.y_ref, bf16[512,4096]{1,0:T(8,128)(2,1)} %bitcast.62, bf16[512,512]{1,0:T(8,128)(2,1)} %get-tuple-element.23.c_ref, bf16[8,128,512]{2,1,0:T(8,128)(2,1)} %copy-done.1, bf16[512,128]{1,0:T(8,128)(2,1)} %get-tuple-element.30.lead, f32[1,4096]{1,0:T(1,128)} %bitcast.74), custom_call_target="tpu_custom_call" | custom-call | flops 2000000000 | bytes 20000000 | tf_op jit(solution)/shard_map/finish/pallas_call | solution.py:404
  (14 shorter events, 0.2 us)
Async XLA Ops:
  1.5 16.5 %collective-permute-start = (bf16[3,5120]{1,0:T(4,128)(2,1)S(1)}, bf16[3,5120]{1,0:T(4,128)(2,1)S(1)}, u32[]{:S(2)}, u32[]{:S(2)}) collective-permute-start(bf16[3,5120]{1,0:T(4,128)(2,1)S(1)} %slice_bitcast_fusion), channel_id=1, source_target_pairs={{0,1},{1,2},{2,3},{3,4},{4,5},{5,6},{6,7},{8,9},{9,10},{10,11},{11... | collective-permute-start | bytes 92168 | tf_op jit(solution)/shard_map/ppermute | solution.py:454
  44.0 47.1 %copy-start.3 = (bf16[128,4096]{1,0:T(8,128)(2,1)S(1)}, bf16[128,4096]{1,0:T(8,128)(2,1)}, u32[]{:S(2)}) copy-start(bf16[128,4096]{1,0:T(8,128)(2,1)} %param.24) | copy-start | bytes 3145732
  44.1 58.3 %copy-start.4 = (bf16[4,4,4096]{2,1,0:T(4,128)(2,1)S(1)}, bf16[4,4,4096]{2,1,0:T(4,128)(2,1)}, u32[]{:S(2)}) copy-start(bf16[4,4,4096]{2,1,0:T(4,128)(2,1)} %param.25) | copy-start | bytes 393220
  44.1 35.6 %all-to-all-start = ((bf16[8,144,512]{2,1,0:T(8,128)(2,1)}), bf16[8,144,512]{2,1,0:T(8,128)(2,1)S(1)}, u32[]{:S(2)}, u32[]{:S(2)}) async-start(bf16[8,144,512]{2,1,0:T(8,128)(2,1)} %get-tuple-element.28), calls=%async_computation | async-start | bytes 2359296 | tf_op jit(solution)/shard_map/all_to_all | solution.py:424
  52.5 76.3 %copy-start.5 = (f32[4096]{0:T(1024)S(1)}, f32[4096]{0:T(1024)}, u32[]{:S(2)}) copy-start(f32[4096]{0:T(1024)} %param.26) | copy-start | bytes 49156
  79.7 1.0 copy-start
  87.6 10.8 %all-to-all-start.3 = ((f32[32,4,128]{2,1,0:T(4,128)}), f32[32,4,128]{2,1,0:T(4,128)S(1)}, u32[]{:S(2)}, u32[]{:S(2)}) async-start(f32[32,4,128]{2,1,0:T(4,128)} %bitcast_dynamic-update-slice_fusion), calls=%async_computation.3 | async-start | bytes 131072 | tf_op jit(solution)/shard_map/all_to_all | solution.py:424
  99.7 16.1 %all-to-all-start.4 = ((f32[32,24,128]{2,1,0:T(8,128)}), f32[32,24,128]{2,1,0:T(8,128)S(1)}, u32[]{:S(2)}, u32[]{:S(2)}) async-start(f32[32,24,128]{2,1,0:T(8,128)} %pad_maximum_fusion), calls=%async_computation.4 | async-start | bytes 786432 | tf_op jit(solution)/shard_map/all_to_all | solution.py:424
  128.8 24.2 %copy-start.2 = (bf16[8,2,128,512]{3,2,1,0:T(8,128)(2,1)S(1)}, bf16[8,2,128,512]{3,2,1,0:T(8,128)(2,1)}, u32[]{:S(2)}) copy-start(bf16[8,2,128,512]{3,2,1,0:T(8,128)(2,1)} %get-tuple-element.32) | copy-start | bytes 6291460
  204.6 29.2 %all-to-all-start.1 = ((bf16[8,128,512]{2,1,0:T(8,128)(2,1)}), bf16[8,128,512]{2,1,0:T(8,128)(2,1)S(1)}, u32[]{:S(2)}, u32[]{:S(2)}) async-start(bf16[8,128,512]{2,1,0:T(8,128)(2,1)} %get-tuple-element.29), calls=%async_computation.1 | async-start | bytes 2097152 | tf_op jit(solution)/shard_map/all_to_all | solution.py:424
  233.9 1.1 copy-start.1

commit v2 on v1

v2 whole, which is shorter than its diff:
```python
import functools
import math

import jax
import jax.numpy as jnp
from jax import lax
from jax.experimental import pallas as pl
from jax.experimental.pallas import tpu as pltpu
from jax.sharding import PartitionSpec as P

D = 4096
HEADS = 64
WIDTH = 64
GROUPS = 4
STATE = 128
KERNEL = 4
SEQS = 4
INNER = HEADS * WIDTH
PER = HEADS // GROUPS
GW = INNER // GROUPS
Q = 128
EXTRA = 16
TINY_FLOOR = 1e-05
LOG2E = 1.0 / math.log(2.0)
BF = jnp.bfloat16
F32 = jnp.float32
HI = lax.Precision.HIGHEST
VM = 56 * 1024 * 1024


def params():
    return pltpu.CompilerParams(vmem_limit_bytes=VM)


def dot(a, b):
    return jnp.dot(a, b, preferred_element_type=F32)


def halves(x):
    hi = x.astype(BF)
    return hi, (x - hi.astype(F32)).astype(BF)


def spread(first_head, width):
    head = lax.broadcasted_iota(jnp.int32, (2 * HEADS, width), 0) % HEADS
    channel = lax.broadcasted_iota(jnp.int32, (2 * HEADS, width), 1)
    return (head == first_head + channel // WIDTH).astype(F32).astype(BF)


def silu(x):
    half = 0.5 * x
    return half + half * jnp.tanh(half)


def stops(lengths, me, T):
    total, ends = -me[0] * T, []
    for k in range(SEQS):
        total = total + lengths[k]
        ends.append(total)
    return ends


def segment(place, ends):
    return sum([(place >= ends[k]).astype(jnp.int32) for k in range(SEQS - 1)])


def prep_kernel(lengths, me, raw_ref, bias_ref, log_ref, gain_ref, a_ref, b_ref, wst_ref, leadj_ref, lead0_ref, pick_ref, small_ref, cum, lj, l0, rows):
    T = raw_ref.shape[1]
    ends = stops(lengths, me, T)
    z = raw_ref[...] + jnp.broadcast_to(bias_ref[...], (8, HEADS)).T[:, 0:1]
    u = jnp.exp(-jnp.abs(z))
    series = u * (1.0 - u * (0.5 - u * (1.0 / 3.0 - u * (0.25 - u * 0.2))))
    dt_t = jnp.maximum(z, 0.0) + jnp.where(u < 0.03, series, jnp.log(1.0 + u))
    dec = -jnp.exp(jnp.broadcast_to(log_ref[...], (8, HEADS)).T[:, 0:1]) * dt_t
    earlier = lax.broadcasted_iota(jnp.int32, (T, T), 0)
    later = lax.broadcasted_iota(jnp.int32, (T, T), 1)
    total_t = jnp.dot(dec, (later >= earlier).astype(F32), precision=HI, preferred_element_type=F32)
    b_ref[...] = (total_t - jnp.log(dt_t)) * LOG2E
    total, dt = total_t.T, dt_t.T
    cum[...] = total
    a2 = total * LOG2E
    for g in range(GROUPS):
        a_ref[g] = a2[:, g * PER : (g + 1) * PER]
    place = lax.broadcasted_iota(jnp.int32, (T, HEADS), 0)
    seg = segment(place, ends)
    lead0 = jnp.where(seg == segment(-1, ends), jnp.exp(total), 0.0)
    l0[...] = lead0
    target = lax.broadcasted_iota(jnp.int32, (Q, Q + 16), 0)
    source = lax.broadcasted_iota(jnp.int32, (Q, Q + 16), 1) - 16
    for j in range(T // Q):
        same = segment(j * Q + target, ends) == segment(j * Q + source, ends)
        for k in range(KERNEL - 1):
            chosen = same & (source == target + (k - (KERNEL - 1)))
            pick_ref[j, k * Q : (k + 1) * Q] = chosen.astype(F32).astype(BF)
    at_stop = [cum[pl.ds(jnp.clip(ends[r] - 1, 0, T - 1), 1), :] for r in range(SEQS)]
    for j in range(T // Q):
        lo, hi = j * Q, (j + 1) * Q
        part = total[lo:hi]
        aim = jnp.broadcast_to(total[hi - 1 : hi], (Q, HEADS))
        for r in range(SEQS - 1):
            aim = jnp.where((seg[lo:hi] == r) & (ends[r] < hi), at_stop[r], aim)
        weight = jnp.exp(aim - part) * dt[lo:hi]
        wst_ref[lo:hi] = jnp.concatenate(halves(weight), axis=1)
        base = total[lo - 1 : lo] if j else 0.0
        lead = jnp.where(seg[lo:hi] == segment(lo - 1, ends), jnp.exp(part - base), 0.0)
        lj[lo:hi] = lead
        rows[j : j + 1] = lead[Q - 1 :]
    leadj_ref[...] = jnp.concatenate(halves(lj[...]), axis=1)
    lead0_ref[...] = jnp.concatenate(halves(lead0), axis=1)
    n = T // Q
    for r in range(SEQS):
        stop = ends[r] - 1
        owned = ((stop >= 0) & (stop < T)).astype(F32)
        at = pl.ds(jnp.clip(stop, 0, T - 1), 1)
        rows[n + r : n + r + 1] = lj[at, :] * owned
        rows[n + SEQS + r : n + SEQS + r + 1] = l0[at, :] * owned
    rows[n + 2 * SEQS : n + 2 * SEQS + 1] = lead0[T - 1 :]
    rows[n + 2 * SEQS + 1 : n + 2 * SEQS + 2] = gain_ref[...]
    small_ref[...] = jnp.concatenate(halves(rows[...]), axis=1)


SMEM = pl.BlockSpec(memory_space=pltpu.SMEM)
VMEM = pl.BlockSpec(memory_space=pltpu.VMEM)


def prep(lengths, me, raw, bias, decay_log, gain):
    T = raw.shape[1]
    nrows = -(-(T // Q + 2 * SEQS + 2) // 16) * 16
    sds = jax.ShapeDtypeStruct
    return pl.pallas_call(
        prep_kernel,
        in_specs=[SMEM, SMEM] + [VMEM] * 4,
        out_specs=[VMEM] * 7,
        out_shape=[
            sds((GROUPS, T, PER), F32),
            sds((HEADS, T), F32),
            sds((T, 2 * HEADS), BF),
            sds((T, 2 * HEADS), BF),
            sds((T, 2 * HEADS), BF),
            sds((T // Q, (KERNEL - 1) * Q, Q + 16), BF),
            sds((nrows, 2 * HEADS), BF),
        ],
        scratch_shapes=[
            pltpu.VMEM((T, HEADS), F32),
            pltpu.VMEM((T, HEADS), F32),
            pltpu.VMEM((T, HEADS), F32),
            pltpu.VMEM((nrows, HEADS), F32),
        ],
        compiler_params=params(),
        name="prep",
    )(lengths, me, raw, bias, decay_log, gain)


def front_kernel(seqs, shard_w, lengths, me, x_ref, b_ref, c_ref, hx, hb, hc, wx, wb, wc, bx, bb, bc, wst, pick, small, gate,
                 xm, bm, cm, pay, eloc, keep0, keep1, give0, give1, act, ent, exs, near, sems):
    slots = ((keep0, keep1), (give0, give1))
    T = x_ref.shape[0]
    n = T // Q
    g = pl.program_id(0)
    ends = stops(lengths, me, T)
    span = me[0]
    shards = GW // shard_w
    cuts = [slice(k * shard_w, (k + 1) * shard_w) for k in range(shards)]
    R = spread(g * PER, GW)
    wide = dot(small[...], R)
    packed = small[...].astype(F32)
    gain = wide[n + 2 * SEQS + 1 : n + 2 * SEQS + 2]
    pieces = [
        (x_ref, hx, wx, bx, xm, 0, GW),
        (b_ref, hb, wb, bb, bm, GW, STATE),
        (c_ref, hc, wc, bc, cm, GW + STATE, STATE),
    ]
    spots = [jnp.clip(ends[r] - 1, 0, T - 1) for r in range(SEQS)]

    def fetch(r):
        top = pl.multiple_of(spots[r] // 16 * 16, 16)
        cols = pl.ds(pl.multiple_of(g * GW, GW), GW)
        return pltpu.make_async_copy(gate.at[pl.ds(top, 16), cols], near.at[r], sems.at[r])

    for r in range(SEQS):
        fetch(r).start()
    ent[...] = jnp.zeros_like(ent)
    for slot in slots[0] + slots[1]:
        slot[...] = jnp.zeros_like(slot)
    exs[...] = jnp.zeros_like(exs)
    for k in range(shards):
        exs[k, 3 * SEQS : 3 * SEQS + 1, 0:128] = packed[n + 2 * SEQS : n + 2 * SEQS + 1]

    for j in range(n):
        lo = j * Q
        for src, halo, w_ref, bias, out, at, w in pieces:
            own = src[lo : lo + Q]
            window = jnp.concatenate([src[lo - 16 : lo] if j else halo[...], own], axis=0)
            for c in range(0, w, 256):
                c2 = min(c + 256, w)
                near3 = dot(pick[j], window[:, c:c2])
                acc = bias[:, c:c2] + w_ref[KERNEL - 1 : KERNEL, c:c2] * own[:, c:c2].astype(F32)
                for k in range(KERNEL - 1):
                    acc = acc + w_ref[k : k + 1, c:c2] * near3[k * Q : (k + 1) * Q]
                y = silu(acc)
                act[lo : lo + Q, at + c : at + c2] = y
                out[lo : lo + Q, c:c2] = y.astype(BF)
        scaled = act[lo : lo + Q, :GW] * dot(wst[lo : lo + Q], R)
        xhi, xlo = halves(scaled)
        right = jnp.concatenate([xhi, xlo, xhi], axis=0)
        bt = act[lo : lo + Q, GW : GW + STATE].T
        lane_seg = segment(lo + lax.broadcasted_iota(jnp.int32, (STATE, Q), 1), ends)

        def gathered(which, bt=bt, lane_seg=lane_seg, right=right):
            bhi, blo = halves(jnp.where(lane_seg == which, bt, 0.0))
            return dot(jnp.concatenate([bhi, bhi, blo], axis=1), right)

        if j:
            eloc[j - 1] = ent[...].astype(BF)
        for r in range(SEQS):
            stop = ends[r] - 1

            @pl.when((stop >= lo) & (stop < lo + Q))
            def _(r=r, stop=stop, gathered=gathered):
                tail = wide[n + r : n + r + 1] * ent[...] + gathered(r)
                if r < SEQS - 1:
                    fits = stop < T - 1
                    if r != 1:
                        fits = fits & ((span < seqs // 2) if r == 0 else (span >= seqs // 2))
                    for p in range(2):

                        @pl.when(fits & (span % 2 == p))
                        def _(p=p):
                            for k in range(shards):
                                to = slots[0 if k % 2 == p else 1][r % 2]
                                to[k // 2] = tail[:, cuts[k]].astype(BF)

                row = act[pl.ds(stop, 1), :].astype(BF)
                out_map = jnp.broadcast_to(row[:, GW + STATE :], (16, STATE))
                thi, tlo = halves(tail)
                value = (dot(out_map, thi) + dot(out_map, tlo))[0:1]
                value = value + gain * row[:, :GW].astype(F32)
                for k in range(shards):
                    exs[k, r : r + 1, :] = value[:, cuts[k]]
                    exs[k, 2 * SEQS + r : 2 * SEQS + r + 1, 0:128] = row[:, GW + STATE :].astype(F32)
                    exs[k, 2 * SEQS + r : 2 * SEQS + r + 1, 128:256] = packed[n + SEQS + r : n + SEQS + r + 1]

        ent[...] = wide[j : j + 1] * ent[...] + gathered(segment(lo + Q - 1, ends))
    for r in range(SEQS):
        fetch(r).wait()
        mine = lax.broadcasted_iota(jnp.int32, (16, GW), 0) == spots[r] % 16
        owned = (spots[r] == ends[r] - 1).astype(F32)
        line = jnp.sum(jnp.where(mine, near[r].astype(F32), 0.0), axis=0, keepdims=True) * owned
        for k in range(shards):
            exs[k, SEQS + r : SEQS + r + 1, :] = line[:, cuts[k]]
    for k in range(shards):
        pay[k, 0:STATE, :] = ent[:, cuts[k]].astype(BF)
        pay[k, STATE:, :] = exs[k].astype(BF)


def front(lengths, me, rows, halo, conv_weight, bias, wst, pick, small, gate, seqs):
    T = rows.shape[0]
    shard_w = INNER // seqs
    shards = GW // shard_w
    n = T // Q
    first_b, first_c = INNER // STATE, INNER // STATE + GROUPS
    sds = jax.ShapeDtypeStruct

    def three(height):
        return [
            pl.BlockSpec((height, GW), lambda g: (0, g)),
            pl.BlockSpec((height, STATE), lambda g: (0, first_b + g)),
            pl.BlockSpec((height, STATE), lambda g: (0, first_c + g)),
        ]

    whole = lambda a: pl.BlockSpec(a.shape, lambda g: (0, 0))
    return pl.pallas_call(
        functools.partial(front_kernel, seqs, shard_w),
        grid=(GROUPS,),
        in_specs=[SMEM, SMEM]
        + three(T)
        + three(16)
        + three(KERNEL)
        + three(1)
        + [whole(wst), pl.BlockSpec(pick.shape, lambda g: (0, 0, 0)), whole(small), pl.BlockSpec(memory_space=pl.ANY)],
        out_specs=[
            pl.BlockSpec((T, GW), lambda g: (0, g)),
            pl.BlockSpec((T, STATE), lambda g: (0, g)),
            pl.BlockSpec((T, STATE), lambda g: (0, g)),
            pl.BlockSpec((shards, STATE + EXTRA, shard_w), lambda g: (g, 0, 0)),
            pl.BlockSpec((n - 1, STATE, GW), lambda g: (0, 0, g)),
        ]
        + [pl.BlockSpec((shards // 2, STATE, shard_w), lambda g: (g, 0, 0))] * 4,
        out_shape=[
            sds((T, INNER), BF),
            sds((T, GROUPS * STATE), BF),
            sds((T, GROUPS * STATE), BF),
            sds((seqs, STATE + EXTRA, shard_w), BF),
            sds((n - 1, STATE, INNER), BF),
        ]
        + [sds((seqs // 2, STATE, shard_w), BF)] * 4,
        scratch_shapes=[
            pltpu.VMEM((T, GW + 2 * STATE), F32),
            pltpu.VMEM((STATE, GW), F32),
            pltpu.VMEM((shards, EXTRA, shard_w), F32),
            pltpu.VMEM((SEQS, 16, GW), BF),
            pltpu.SemaphoreType.DMA((SEQS,)),
        ],
        compiler_params=params(),
        name="front",
    )(lengths, me, rows, rows, rows, halo, halo, halo, conv_weight, conv_weight, conv_weight, bias, bias, bias, wst, pick, small, gate)


def local_kernel(gain_row, lengths, me, x_ref, b_ref, c_ref, a_ref, bt_ref, lead, eloc, small, out):
    T = x_ref.shape[0]
    ends = stops(lengths, me, T)
    R = spread(pl.program_id(0) * PER, GW)
    wide = dot(small[...], R)
    gain = wide[gain_row : gain_row + 1]
    low = (lax.broadcasted_iota(jnp.int32, (Q, 2 * WIDTH), 1) < WIDTH).astype(F32).astype(BF)
    high = 1 - low
    for j in range(T // Q):
        lo = j * Q
        span = slice(lo, lo + Q)
        t = lo + lax.broadcasted_iota(jnp.int32, (Q, Q), 0)
        s = lo + lax.broadcasted_iota(jnp.int32, (Q, Q), 1)
        out_map = c_ref[span]
        scores = lax.dot_general(out_map, b_ref[span], (((1,), (1,)), ((), ())), preferred_element_type=F32)
        scores = jnp.where((s <= t) & (segment(t, ends) == segment(s, ends)), scores, 0.0)
        a, b = a_ref[0, span], bt_ref[:, span]
        if j:
            base = dot(lead[span], R) * dot(out_map, eloc[j - 1])
        for p in range(PER // 2):
            col = slice(2 * p * WIDTH, 2 * (p + 1) * WIDTH)
            m = [
                (jnp.exp2(jnp.minimum(a[:, h : h + 1] - b[h : h + 1, :], 60.0)) * scores).astype(BF)
                for h in (2 * p, 2 * p + 1)
            ]
            x = x_ref[span, col]
            y = dot(jnp.concatenate(m, axis=1), jnp.concatenate([x * low, x * high], axis=0))
            y = y + gain[:, col] * x.astype(F32)
            out[span, col] = y + base[:, col] if j else y


def local(lengths, me, xm, bm, cm, a2, b2, lead, eloc, small):
    T = xm.shape[0]
    n = T // Q
    return pl.pallas_call(
        functools.partial(local_kernel, n + 2 * SEQS + 1),
        grid=(GROUPS,),
        in_specs=[
            SMEM,
            SMEM,
            pl.BlockSpec((T, GW), lambda g: (0, g)),
            pl.BlockSpec((T, STATE), lambda g: (0, g)),
            pl.BlockSpec((T, STATE), lambda g: (0, g)),
            pl.BlockSpec((1, T, PER), lambda g: (g, 0, 0)),
            pl.BlockSpec((PER, T), lambda g: (g, 0)),
            pl.BlockSpec((T, 2 * HEADS), lambda g: (0, 0)),
            pl.BlockSpec((n - 1, STATE, GW), lambda g: (0, 0, g)),
            pl.BlockSpec(small.shape, lambda g: (0, 0)),
        ],
        out_specs=pl.BlockSpec((T, GW), lambda g: (0, g)),
        out_shape=jax.ShapeDtypeStruct((T, INNER), F32),
        compiler_params=params(),
        cost_estimate=pl.CostEstimate(flops=8 * 10**9, bytes_accessed=2 * 10**7, transcendentals=5 * 10**6),
        name="local",
    )(lengths, me, xm, bm, cm, a2, b2, lead, eloc, small)


def scan_kernel(T, lengths, me, got, enter, base, mail, value, ent):
    seqs, _, shard_w = got.shape
    _, _, share = mail.shape
    ends = stops(lengths, me, T)
    R = spread(me[0] * (shard_w // WIDTH), shard_w)
    ent[...] = jnp.zeros_like(ent)
    mail[...] = jnp.zeros_like(mail)
    for i in range(seqs):
        now = ent[...]
        enter[i] = now.astype(BF)
        state = got[i, 0:STATE].astype(F32)
        extra = got[i, STATE:]
        carry = dot(extra[:, 0:128], R)[3 * SEQS : 3 * SEQS + 1]
        for r in range(SEQS):
            stop = ends[r] + (me[0] - i) * T

            @pl.when((stop > 0) & (stop <= T))
            def _(r=r, now=now, state=state, extra=extra, stop=stop):
                at = slice(2 * SEQS + r, 2 * SEQS + r + 1)
                lead = dot(extra[:, 128:256], R)[at]
                base[r] = lead * now + jnp.where(stop == T, state, 0.0)
                hi, lo = halves(now)
                inter = (dot(extra[:, 0:128], hi) + dot(extra[:, 0:128], lo))[at]
                rows = extra.astype(F32)
                value[r : r + 1, :] = (rows[r : r + 1] + lead * inter) * silu(rows[SEQS + r : SEQS + r + 1])

        ent[...] = carry * now + state
    parts = shard_w // share
    v = value[0:SEQS]
    squares = jnp.broadcast_to(jnp.sum(v * v, axis=1, keepdims=True), (SEQS, share))
    for k in range(mail.shape[0]):
        mail[k, SEQS:] = squares
    for k in range(parts):
        mail[me[0] * parts + k, 0:SEQS] = value[0:SEQS, k * share : (k + 1) * share]


def scan(lengths, me, T, got, devices, share):
    seqs, _, shard_w = got.shape
    sds = jax.ShapeDtypeStruct
    return pl.pallas_call(
        functools.partial(scan_kernel, T),
        in_specs=[SMEM, SMEM, VMEM],
        out_specs=[VMEM] * 3,
        out_shape=[
            sds((seqs, STATE, shard_w), BF),
            sds((SEQS, STATE, shard_w), F32),
            sds((devices, 2 * SEQS, share), F32),
        ],
        scratch_shapes=[pltpu.VMEM((8, shard_w), F32), pltpu.VMEM((STATE, shard_w), F32)],
        compiler_params=params(),
        name="scan",
    )(lengths, me, got)


def finals_kernel(T, lengths, me, base, *refs):
    out = refs[-1]
    count = len(refs) - 1
    ends = stops(lengths, me, T)
    for r in range(SEQS):
        out[r] = base[r].T
        if r == SEQS - 1:
            continue
        last = ends[r] + me[0] * T - 1
        for c in range(count):

            @pl.when((last % T != T - 1) & ((last // (2 * T)) ^ (me[0] // 2) == c))
            def _(r=r, c=c):
                out[r] = (base[r] + refs[c][r % 2].astype(F32)).T


def finals(lengths, me, T, base, pieces):
    _, _, shard_w = base.shape
    return pl.pallas_call(
        functools.partial(finals_kernel, T),
        in_specs=[SMEM, SMEM] + [VMEM] * (1 + len(pieces)),
        out_specs=VMEM,
        out_shape=jax.ShapeDtypeStruct((SEQS, shard_w, STATE), F32),
        compiler_params=params(),
        name="finals",
    )(lengths, me, base, *pieces)


def finish_kernel(y_ref, gate, c_ref, e_ref, lead, norm, out):
    R = spread(pl.program_id(0) * PER, GW)
    entering = jnp.concatenate([e_ref[k] for k in range(e_ref.shape[0])], axis=1)
    y = y_ref[...] + dot(lead[...], R) * dot(c_ref[...], entering)
    v = y * silu(gate[...].astype(F32))
    scale = lax.rsqrt(jnp.sum(v * v, axis=1, keepdims=True) * (1.0 / GW) + TINY_FLOOR)
    out[...] = (v * scale * norm[...]).astype(BF)


def finish(y_local, gate, cm, enter, lead, norm):
    T = y_local.shape[0]
    seqs, _, shard_w = enter.shape
    tile = T
    return pl.pallas_call(
        finish_kernel,
        grid=(GROUPS, T // tile),
        in_specs=[
            pl.BlockSpec((tile, GW), lambda g, i: (i, g)),
            pl.BlockSpec((tile, GW), lambda g, i: (i, g)),
            pl.BlockSpec((tile, STATE), lambda g, i: (i, g)),
            pl.BlockSpec((GW // shard_w, STATE, shard_w), lambda g, i: (g, 0, 0)),
            pl.BlockSpec((tile, 2 * HEADS), lambda g, i: (i, 0)),
            pl.BlockSpec((1, GW), lambda g, i: (0, g)),
        ],
        out_specs=pl.BlockSpec((tile, GW), lambda g, i: (i, g)),
        out_shape=jax.ShapeDtypeStruct((T, INNER), BF),
        compiler_params=params(),
        cost_estimate=pl.CostEstimate(flops=2 * 10**9, bytes_accessed=2 * 10**7, transcendentals=4 * 10**6),
        name="finish",
    )(y_local, gate, cm, enter, lead, norm)


def largest_kernel(h_ref, w_ref, out):
    logits = lax.dot_general(w_ref[...], h_ref[...], (((1,), (1,)), ((), ())), preferred_element_type=F32)
    top = jnp.max(logits, axis=0, keepdims=True)
    first = pl.program_id(0) == 0
    out[...] = jnp.where(first, top, jnp.maximum(top, out[...]))


def largest(normed, vocab_weight):
    count, depth = normed.shape
    height = 1024
    return pl.pallas_call(
        largest_kernel,
        grid=(vocab_weight.shape[0] // height,),
        in_specs=[
            pl.BlockSpec((count, depth), lambda i: (0, 0)),
            pl.BlockSpec((height, depth), lambda i: (i, 0)),
        ],
        out_specs=pl.BlockSpec((1, count), lambda i: (0, 0)),
        out_shape=jax.ShapeDtypeStruct((1, count), F32),
        compiler_params=params(),
        name="largest",
    )(normed, vocab_weight)


def swap(x, seqs, distance):
    return lax.ppermute(x, "seq", [(i, i ^ distance) for i in range(seqs)])


def exchange(x, axes):
    return lax.all_to_all(x, axes, 0, 0, tiled=True)


def body(
    conv_input,
    gate_projected,
    step_raw,
    step_bias,
    decay_log,
    head_direct_gain,
    conv_weight,
    convolution_bias,
    norm_weight,
    lengths,
    out_weight,
    residual_last,
    final_gain,
    vocab_weight,
):
    every = ("req", "seq")
    T = conv_input.shape[1]
    seqs, reqs = lax.axis_size("seq"), lax.axis_size("req")
    seq_place, req_place = lax.axis_index("seq"), lax.axis_index("req")
    devices = seqs * reqs
    flat = req_place * seqs + seq_place
    shard_w = INNER // seqs
    share = out_weight.shape[0]
    rows_total = reqs * SEQS
    rows = conv_input[0]

    edge = lax.ppermute(rows[T - (KERNEL - 1) :], "seq", [(i, i + 1) for i in range(seqs - 1)])
    halo = jnp.pad(edge, ((16 - (KERNEL - 1), 0), (0, 0)))
    me = seq_place[None].astype(jnp.int32)
    lens = lengths[0].astype(jnp.int32)
    a2, b2, wst, leadj, lead0, pick, small = prep(
        lens, me, step_raw[0].T, step_bias[None], decay_log[None], head_direct_gain[None]
    )
    xm, bm, cm, pay, eloc, *slots = front(
        lens, me, rows, halo, conv_weight, convolution_bias[None], wst, pick, small, gate_projected[0], seqs
    )
    got = exchange(pay, "seq")
    y_local = local(lens, me, xm, bm, cm, a2, b2, leadj, eloc, small)
    got, y_local = lax.optimization_barrier((got, y_local))
    enter, base, mail = scan(lens, me, T, got, devices, share)

    mail, slots = lax.optimization_barrier((mail, slots))
    given = [swap(slots[2], seqs, 1)]
    mail = exchange(mail, every)
    mail, given, kept = lax.optimization_barrier((mail, given, slots[3]))
    given.append(swap(kept, seqs, 1))
    mail = mail.reshape(reqs, seqs, 2 * SEQS, share)
    v = lax.dynamic_index_in_dim(mail[:, :, :SEQS], flat * share // shard_w, 1, keepdims=False)
    near = GW // shard_w
    squares = lax.dynamic_slice_in_dim(mail[:, :, SEQS:], flat * share // GW * near, near, 1).sum(axis=1)
    v = v * lax.rsqrt(squares * (1.0 / GW) + TINY_FLOOR)
    u = (v * lax.dynamic_slice_in_dim(norm_weight, flat * share, share)).astype(BF).reshape(rows_total, share)
    partial = jnp.dot(u, out_weight, preferred_element_type=F32)
    chunk = D // devices
    mail = exchange(partial.reshape(rows_total, devices, chunk).transpose(1, 0, 2), every)
    own = mail.sum(axis=0)
    residual = residual_last.reshape(rows_total, D)
    own = own + lax.dynamic_slice_in_dim(residual, flat * chunk, chunk, 1).astype(F32)
    mail = exchange(jnp.broadcast_to(own.astype(BF), (devices, rows_total, chunk)), every).astype(F32)
    hidden = mail.transpose(1, 0, 2).reshape(rows_total, D)
    hidden, enter = lax.optimization_barrier((hidden, enter))
    entering = exchange(enter, "seq")
    rms = lax.rsqrt(jnp.mean(hidden * hidden, axis=-1, keepdims=True) + TINY_FLOOR)
    normed = (hidden * rms * final_gain).astype(BF)
    last_hidden = lax.dynamic_slice_in_dim(hidden.reshape(reqs, SEQS, D), req_place, 1, 0).astype(BF)
    top = largest(normed, vocab_weight).reshape(reqs, 1, SEQS)
    top = jnp.broadcast_to(top, (reqs, seqs, SEQS)).reshape(devices, SEQS)
    top, entering, given = lax.optimization_barrier((top, entering, given))

    pair = seq_place // 2
    tails = [
        jnp.stack([
            lax.dynamic_index_in_dim(kept, pair ^ c, 0, keepdims=False) + lax.dynamic_index_in_dim(other, pair ^ c, 0, keepdims=False)
            for kept, other in zip(slots[:2], given)
        ])
        for c in range(seqs // 2)
    ]
    tails, entering = lax.optimization_barrier((tails, entering))
    tails = [tails[0]] + [swap(tails[c], seqs, 2 * c) for c in range(1, seqs // 2)]
    y_gated = finish(y_local, gate_projected[0], cm, entering, lead0, norm_weight[None])

    max_logit = jnp.max(exchange(top, every), axis=0, keepdims=True)
    final_states = finals(lens, me, T, base, tails).reshape(1, SEQS, HEADS // seqs, WIDTH, STATE)
    return (y_gated[None], final_states, last_hidden, max_logit)


def solution(mesh):
    return jax.shard_map(
        body,
        mesh=mesh,
        in_specs=(
            P("req", "seq", None),
            P("req", "seq", None),
            P("req", "seq", None),
            P(),
            P(),
            P(),
            P(),
            P(),
            P(),
            P("req", None),
            P(("req", "seq"), None),
            P(),
            P(),
            P(("req", "seq"), None),
        ),
        out_specs=(
            P("req", "seq", None),
            P("req", None, "seq", None, None),
            P("req", None, None),
            P("req", None),
        ),
        check_vma=False,
    )
```

time: 248 us -> 174 us (0.70)
  blocking collectives: 73.5 us -> 9.9 us
  matrix products: 15.2 us -> 1.09 us
  starting transfers between devices: 22.4 us -> 34.5 us
  local copies, waits for them, and re-layouts: 12.5 us -> 7.24 us
    all_to_all x3 -> x1, blocking collectives: 73.5 us -> 9.9 us  [exchange(): return lax.all_to_all(x, axes, 0, 0, tiled=True)]
    dot_general x1 -> x0, matrix products: 14.8 us -> none  [body(): lax.dot_general(normed, vocab_weight, (((1,), (1,)), ((), ())), preferred...]
    ppermute x0 -> x5, starting transfers between devices: none -> 7.51 us  [swap(): return lax.ppermute(x, 'seq', [(i, i ^ distance) for i in range(seqs)])]
    pallas_call x4 -> x5, Pallas kernels: 31.6 us -> 37.7 us  [the longest x1 14.7 us: largest(): pl.pallas_call(largest_kernel, grid=(vocab_weight.shape[0] // height,), i...]
    pallas_call x1, Pallas kernels: 25.3 us -> 19.2 us  [front(): pl.pallas_call(functools.partial(front_kernel, seqs, shard_w), grid=(GROU...]
    ppermute x0 -> x5, waiting for transfers between devices: none -> 5.56 us  [swap(): return lax.ppermute(x, 'seq', [(i, i ^ distance) for i in range(seqs)])]
    all_to_all x4 -> x5, waiting for transfers between devices: 47.6 us -> 42.3 us  [exchange(): return lax.all_to_all(x, axes, 0, 0, tiled=True)]
    all_to_all x4 -> x5, starting transfers between devices: 17.5 us -> 22.1 us  [exchange(): return lax.all_to_all(x, axes, 0, 0, tiled=True)]
  transfers between devices with their start and end apart: 5 -> 11, of which waited for: 4 -> 6; matrix products, arithmetic and copies ran while one was open for 5% -> 4% of each run, Pallas kernels for 11% -> 23%
where the time goes in v2:
time: 174 us; the launch traced here: 173 us
  Pallas kernels  67.4 us (39%)
  waiting for transfers between devices  47.9 us (28%)
  starting transfers between devices  34.5 us (20%)
  blocking collectives  9.9 us (6%)
  local copies, waits for them, and re-layouts  7.24 us (4%)
  other arithmetic  3.91 us (2%)
    all_to_all x5, waiting for transfers between devices, exchange(): return lax.all_to_all(x, axes, 0, 0, tiled=True)  42.3 us
    all_to_all x5, starting transfers between devices, exchange(): return lax.all_to_all(x, axes, 0, 0, tiled=True)  22.1 us
    pallas_call x1, Pallas kernels, front(): pl.pallas_call(functools.partial(front_kernel, seqs, shard_w), grid=(GROU...  19.2 us
    pallas_call x1, Pallas kernels, largest(): pl.pallas_call(largest_kernel, grid=(vocab_weight.shape[0] // height,), i...  14.7 us
    pallas_call x1, Pallas kernels, local(): pl.pallas_call(functools.partial(local_kernel, n + 2 * SEQS + 1), grid=(G...  11.1 us
    pallas_call x1, Pallas kernels, finish(): pl.pallas_call(finish_kernel, grid=(GROUPS, T // tile), in_specs=[pl.Bloc...  10.5 us
    all_to_all x1, blocking collectives, exchange(): return lax.all_to_all(x, axes, 0, 0, tiled=True)  9.9 us
    ppermute x5, starting transfers between devices, swap(): return lax.ppermute(x, 'seq', [(i, i ^ distance) for i in range(seqs)])  7.51 us
  transfers between devices with their start and end apart: 11, of which 6 were waited for; matrix products, arithmetic and copies ran while one was open for 4% of the time, Pallas kernels for 23%

profile of v2, /device:TPU:0, one launch (start us, length us, event | category | flops | bytes accessed | tf_op | source)
XLA Modules:
  0.0 172.9 jit_solution(14320737910578857260)
XLA Ops:
  0.6 0.9 slice_bitcast_fusion
  1.5 4.9 %collective-permute-start = (bf16[3,5120]{1,0:T(4,128)(2,1)S(1)}, bf16[3,5120]{1,0:T(4,128)(2,1)S(1)}, u32[]{:S(2)}, u32[]{:S(2)}) collective-permute-start(bf16[3,5120]{1,0:T(4,128)(2,1)S(1)} %slice_bitcast_fusion), channel_id=1, source_target_pairs={{0,1},{1,2},{2,3},{3,4},{4,5},{5,6},{6,7},{8,9},{9,10},{10,11},{11... | collective-permute-start | bytes 92168 | tf_op jit(solution)/shard_map/ppermute | solution.py:539
  6.4 3.5 %prep.1 = (f32[4,512,16]{2,1,0:T(8,128)}, f32[64,512]{1,0:T(8,128)}, bf16[512,128]{1,0:T(8,128)(2,1)}, bf16[512,128]{1,0:T(8,128)(2,1)}, bf16[512,128]{1,0:T(8,1...) custom-call(s32[4]{0:T(128)} %bitcast.58, s32[1]{0:T(128)} %bitcast.1.me, f32[64,512]{1,0:T(8,128)} %bitcast.55, ...), custom_call_target="tpu_custom_call" | custom-call | tf_op jit(solution)/shard_map/prep/pallas_call | solution.py:130
  10.0 0.0 collective-permute-done
  10.0 0.7 pad.4.hx.hb.hc
  10.7 19.2 %front.1 = (bf16[512,4096]{1,0:T(8,128)(2,1)}, bf16[512,512]{1,0:T(8,128)(2,1)}, bf16[512,512]{1,0:T(8,128)(2,1)}, bf16[8,144,512]{2,1,0:T(8,128)(2,1)}, bf16[3,...) custom-call(s32[4]{0:T(128)} %bitcast.59, ...), custom_call_target="tpu_custom_call" | custom-call | tf_op jit(solution)/shard_map/front/pallas_call | solution.py:272
  29.9 5.9 %all-to-all-start = ((bf16[8,144,512]{2,1,0:T(8,128)(2,1)}), bf16[8,144,512]{2,1,0:T(8,128)(2,1)S(1)}, u32[]{:S(2)}, u32[]{:S(2)}) async-start(bf16[8,144,512]{2,1,0:T(8,128)(2,1)} %get-tuple-element.47), calls=%async_computation | async-start | bytes 2359296 | tf_op jit(solution)/shard_map/all_to_all | solution.py:509
  35.8 0.0 copy-start.10
  35.8 0.0 copy-start.2
  35.8 11.1 %local.1.y_ref = f32[512,4096]{1,0:T(8,128)} custom-call(s32[4]{0:T(128)} %bitcast.60, s32[1]{0:T(128)} %bitcast.1.me, bf16[512,4096]{1,0:T(8,128)(2,1)} %get-tuple-element.48.x_ref, bf16[512,512]{1,0:T(8,128)(2,1)} %get-tuple-element.49.b_ref, bf16[512,512]{1,0:T(8,128)(2,1)} %get-tuple-element.50.c_ref, f32[4,512,16]{2,1,0:T(8,128)} %get-tuple-element.51.a_ref, ...), custom_call_target="tpu_custom_call" | custom-call | flops 8000000000 | bytes 20000000 | tf_op jit(solution)/shard_map/local/pallas_call | solution.py:343
  46.9 16.3 %all-to-all-done.got = bf16[8,144,512]{2,1,0:T(8,128)(2,1)S(1)} async-done(((bf16[8,144,512]{2,1,0:T(8,128)(2,1)}), bf16[8,144,512]{2,1,0:T(8,128)(2,1)S(1)}, u32[]{:S(2)}, u32[]{:S(2)}) %all-to-all-start) | async-done | bytes 1179680 | tf_op jit(solution)/shard_map/all_to_all | solution.py:509
  63.3 1.0 copy-done
  64.3 5.0 %scan.1 = (bf16[8,128,512]{2,1,0:T(8,128)(2,1)}, f32[4,128,512]{2,1,0:T(8,128)}, f32[32,8,128]{2,1,0:T(8,128)}) custom-call(s32[4]{0:T(128)} %bitcast.61, s32[1]{0:T(128)} %bitcast.1.me, bf16[8,144,512]{2,1,0:T(8,128)(2,1)} %copy-done), custom_call_target="tpu_custom_call" | custom-call | tf_op jit(solution)/shard_map/scan/pallas_call | solution.py:405
  69.3 0.0 copy-done.10
  69.3 1.2 collective-permute-start.1
  70.6 3.7 %all-to-all-start.1 = ((f32[32,8,128]{2,1,0:T(8,128)}), f32[32,8,128]{2,1,0:T(8,128)S(1)}, u32[]{:S(2)}, u32[]{:S(2)}) async-start(f32[32,8,128]{2,1,0:T(8,128)} %get-tuple-element.63), calls=%async_computation.1 | async-start | bytes 262144 | tf_op jit(solution)/shard_map/all_to_all | solution.py:509
  74.4 0.0 copy-done.2
  74.4 0.0 copy-start.9
  74.4 0.7 copy.24
  75.1 0.8 dynamic_slice.68
  75.8 7.1 %all-to-all-done.1 = f32[32,8,128]{2,1,0:T(8,128)S(1)} async-done(((f32[32,8,128]{2,1,0:T(8,128)}), f32[32,8,128]{2,1,0:T(8,128)S(1)}, u32[]{:S(2)}, u32[]{:S(2)}) %all-to-all-start.1) | async-done | bytes 131104 | tf_op jit(solution)/shard_map/all_to_all | solution.py:509
  82.9 0.0 collective-permute-done.1
  83.0 1.1 convolution_bitcast_fusion
  84.1 6.0 %all-to-all-start.2 = ((f32[32,16,128]{2,1,0:T(8,128)}), f32[32,16,128]{2,1,0:T(8,128)S(1)}, u32[]{:S(2)}, u32[]{:S(2)}) async-start(f32[32,16,128]{2,1,0:T(8,128)} %convolution_bitcast_fusion), calls=%async_computation.2 | async-start | bytes 524288 | tf_op jit(solution)/shard_map/all_to_all | solution.py:509
  90.1 0.0 copy-done.8
  90.2 10.6 %all-to-all-done.2 = f32[32,16,128]{2,1,0:T(8,128)S(1)} async-done(((f32[32,16,128]{2,1,0:T(8,128)}), f32[32,16,128]{2,1,0:T(8,128)S(1)}, u32[]{:S(2)}, u32[]{:S(2)}) %all-to-all-start.2) | async-done | bytes 262176 | tf_op jit(solution)/shard_map/all_to_all | solution.py:509
  100.9 9.9 %all_to_all.34 = bf16[32,16,128]{2,1,0:T(8,128)(2,1)S(1)} all-to-all(bf16[32,16,128]{2,1,0:T(8,128)(2,1)S(1)} %broadcast_in_dim.42), channel_id=1, replica_groups=mesh['req'=4,'seq'=8] {'req','seq'}, dimensions={0} | all-to-all | bytes 262144 | tf_op jit(solution)/shard_map/all_to_all | solution.py:509
  110.8 3.6 %all-to-all-start.4 = ((bf16[8,128,512]{2,1,0:T(8,128)(2,1)}), bf16[8,128,512]{2,1,0:T(8,128)(2,1)S(1)}, u32[]{:S(2)}, u32[]{:S(2)}) async-start(bf16[8,128,512]{2,1,0:T(8,128)(2,1)} %get-tuple-element.69), calls=%async_computation.4 | async-start | bytes 2097152 | tf_op jit(solution)/shard_map/all_to_all | solution.py:509
  114.4 1.9 %collective-permute-start.2 = (bf16[4,128,512]{2,1,0:T(8,128)(2,1)}, bf16[4,128,512]{2,1,0:T(8,128)(2,1)S(1)}, u32[]{:S(2)}, u32[]{:S(2)}) collective-permute-start(bf16[4,128,512]{2,1,0:T(8,128)(2,1)} %get-tuple-element.71), channel_id=1, source_target_pairs={{0,1},{1,0},{2,3},{3,2},{4,5},{5,4},{6,7},{7,6},{8,9},{9,8},{10,11... | collective-permute-start | bytes 1572872 | tf_op jit(solution)/shard_map/ppermute | solution.py:505
  116.3 0.1 reshape.79
  116.3 0.1 multiply_reduce_fusion
  116.5 0.0 copy-done.9
  116.5 0.8 multiply_convert_fusion.h_ref
  117.3 14.7 %largest.1 = f32[1,16]{1,0:T(1,128)} custom-call(bf16[16,4096]{1,0:T(8,128)(2,1)} %multiply_convert_fusion.h_ref, bf16[4096,4096]{1,0:T(8,128)(2,1)} %w_ref.1), custom_call_target="tpu_custom_call" | custom-call | tf_op jit(solution)/shard_map/largest/pallas_call | solution.py:490
  131.9 0.5 broadcast.56
  132.4 1.3 reduce.4
  133.8 0.1 broadcast_in_dim.43
  133.8 0.1 copy.22
  133.9 0.1 broadcast_in_dim.44
  134.0 0.1 reshape.77
  134.1 5.6 %collective-permute-done.2 = bf16[4,128,512]{2,1,0:T(8,128)(2,1)S(1)} collective-permute-done((bf16[4,128,512]{2,1,0:T(8,128)(2,1)}, bf16[4,128,512]{2,1,0:T(8,128)(2,1)S(1)}, u32[]{:S(2)}, u32[]{:S(2)}) %collective-permute-start.2) | collective-permute-done | bytes 524320 | tf_op jit(solution)/shard_map/ppermute | solution.py:505
  139.6 1.0 all-to-all-done.4.e_ref
  140.6 0.0 copy-done.3
  140.6 0.0 copy-done.4
  140.6 0.1 dynamic-slice_add_fusion
  140.8 0.8 pad_maximum_fusion.refs_0_
  141.7 0.5 collective-permute-start.3
  142.2 2.4 %collective-permute-start.4 = (bf16[2,128,512]{2,1,0:T(8,128)(2,1)S(1)}, bf16[2,128,512]{2,1,0:T(8,128)(2,1)S(1)}, u32[]{:S(2)}, u32[]{:S(2)}) collective-permute-start(bf16[2,128,512]{2,1,0:T(8,128)(2,1)S(1)} %pad_maximum_fusion.2), channel_id=1, source_target_pairs={{0,4},{1,5},{2,6},{3,7},{4,0},{5,1},{6,2},{7,3},{8,12},{9,13},{10,... | collective-permute-start | bytes 786440 | tf_op jit(solution)/shard_map/ppermute | solution.py:505
  144.6 1.5 collective-permute-start.5
  146.1 0.6 dynamic-slice_convert_fusion
  146.7 0.7 copy.23
  147.4 2.9 %all-to-all-start.5 = ((f32[32,1,4]{2,1,0:T(1,128)}), f32[32,1,4]{2,1,0:T(1,128)S(1)}, u32[]{:S(2)}, u32[]{:S(2)}) async-start(f32[32,1,4]{2,1,0:T(1,128)} %copy.23), calls=%async_computation.5 | async-start | bytes 32768 | tf_op jit(solution)/shard_map/all_to_all | solution.py:509
  150.3 0.0 copy-done.1
  150.3 10.5 %finish.1 = bf16[512,4096]{1,0:T(8,128)(2,1)} custom-call(f32[512,4096]{1,0:T(8,128)} %local.1.y_ref, bf16[512,4096]{1,0:T(8,128)(2,1)} %bitcast.46, bf16[512,512]{1,0:T(8,128)(2,1)} %get-tuple-element.50.c_ref, bf16[8,128,512]{2,1,0:T(8,128)(2,1)} %copy-done.1, bf16[512,128]{1,0:T(8,128)(2,1)} %get-tuple-element.77.lead, f32[1,4096]{1,0:T(1,128)} %bitcast.57), custom_call_target="tpu_custom_call" | custom-call | flops 2000000000 | bytes 20000000 | tf_op jit(solution)/shard_map/finish/pallas_call | solution.py:461
  160.7 7.4 %all-to-all-done.5 = f32[32,1,4]{2,1,0:T(1,128)S(1)} async-done(((f32[32,1,4]{2,1,0:T(1,128)}), f32[32,1,4]{2,1,0:T(1,128)S(1)}, u32[]{:S(2)}, u32[]{:S(2)}) %all-to-all-start.5) | async-done | bytes 544 | tf_op jit(solution)/shard_map/all_to_all | solution.py:509
  168.1 0.6 reduce_max.9
  168.7 0.0 collective-permute-done.3.refs_1_
  168.7 0.0 collective-permute-done.4.refs_2_
  168.7 0.0 collective-permute-done.5.refs_3_
  168.7 0.0 copy-start.7
  168.7 0.7 copy-done.5
  169.4 0.1 copy-done.6
  169.5 0.1 copy-done.7
  169.6 3.3 %finals.1 = f32[4,512,128]{2,1,0:T(8,128)} custom-call(s32[4]{0:T(128)} %bitcast.62, s32[1]{0:T(128)} %bitcast.1.me, f32[4,128,512]{2,1,0:T(8,128)} %get-tuple-element.78.base, bf16[2,128,512]{2,1,0:T(8,128)(2,1)} %pad_maximum_fusion.refs_0_, bf16[2,128,512]{2,1,0:T(8,128)(2,1)} %copy-done.5, bf16[2,128,512]{2,1,0:T(8,128)(2,1)} %copy-done.6, ...), custom_call_target="tpu_custom_call" | custom-call | tf_op jit(solution)/shard_map/finals/pallas_call | solution.py:438
  (19 shorter events, 0.3 us)
Async XLA Ops:
  1.5 8.4 %collective-permute-start = (bf16[3,5120]{1,0:T(4,128)(2,1)S(1)}, bf16[3,5120]{1,0:T(4,128)(2,1)S(1)}, u32[]{:S(2)}, u32[]{:S(2)}) collective-permute-start(bf16[3,5120]{1,0:T(4,128)(2,1)S(1)} %slice_bitcast_fusion), channel_id=1, source_target_pairs={{0,1},{1,2},{2,3},{3,4},{4,5},{5,6},{6,7},{8,9},{9,10},{10,11},{11... | collective-permute-start | bytes 92168 | tf_op jit(solution)/shard_map/ppermute | solution.py:539
  29.9 33.4 %all-to-all-start = ((bf16[8,144,512]{2,1,0:T(8,128)(2,1)}), bf16[8,144,512]{2,1,0:T(8,128)(2,1)S(1)}, u32[]{:S(2)}, u32[]{:S(2)}) async-start(bf16[8,144,512]{2,1,0:T(8,128)(2,1)} %get-tuple-element.47), calls=%async_computation | async-start | bytes 2359296 | tf_op jit(solution)/shard_map/all_to_all | solution.py:509
  35.8 33.6 %copy-start.10 = (bf16[4,128,512]{2,1,0:T(8,128)(2,1)S(1)}, bf16[4,128,512]{2,1,0:T(8,128)(2,1)}, u32[]{:S(2)}) copy-start(bf16[4,128,512]{2,1,0:T(8,128)(2,1)} %get-tuple-element.64) | copy-start | bytes 1572868
  35.8 38.6 %copy-start.2 = (bf16[128,4096]{1,0:T(8,128)(2,1)S(1)}, bf16[128,4096]{1,0:T(8,128)(2,1)}, u32[]{:S(2)}) copy-start(bf16[128,4096]{1,0:T(8,128)(2,1)} %param.24) | copy-start | bytes 3145732
  46.9 43.2 %copy-start.8 = (bf16[4,4,4096]{2,1,0:T(4,128)(2,1)S(1)}, bf16[4,4,4096]{2,1,0:T(4,128)(2,1)}, u32[]{:S(2)}) copy-start(bf16[4,4,4096]{2,1,0:T(4,128)(2,1)} %param.25) | copy-start | bytes 393220
  63.3 1.0 copy-start
  69.3 13.6 %collective-permute-start.1 = (bf16[4,128,512]{2,1,0:T(8,128)(2,1)S(1)}, bf16[4,128,512]{2,1,0:T(8,128)(2,1)S(1)}, u32[]{:S(2)}, u32[]{:S(2)}) collective-permute-start(bf16[4,128,512]{2,1,0:T(8,128)(2,1)S(1)} %copy-done.10), channel_id=1, source_target_pairs={{0,1},{1,0},{2,3},{3,2},{4,5},{5,4},{6,7},{7,6},{8,9},{9,8},{10,11... | collective-permute-start | bytes 1572872 | tf_op jit(solution)/shard_map/ppermute | solution.py:505
  70.6 12.3 %all-to-all-start.1 = ((f32[32,8,128]{2,1,0:T(8,128)}), f32[32,8,128]{2,1,0:T(8,128)S(1)}, u32[]{:S(2)}, u32[]{:S(2)}) async-start(f32[32,8,128]{2,1,0:T(8,128)} %get-tuple-element.63), calls=%async_computation.1 | async-start | bytes 262144 | tf_op jit(solution)/shard_map/all_to_all | solution.py:509
  74.4 42.1 %copy-start.9 = (f32[4096]{0:T(1024)S(1)}, f32[4096]{0:T(1024)}, u32[]{:S(2)}) copy-start(f32[4096]{0:T(1024)} %param.26) | copy-start | bytes 49156
  84.1 16.7 %all-to-all-start.2 = ((f32[32,16,128]{2,1,0:T(8,128)}), f32[32,16,128]{2,1,0:T(8,128)S(1)}, u32[]{:S(2)}, u32[]{:S(2)}) async-start(f32[32,16,128]{2,1,0:T(8,128)} %convolution_bitcast_fusion), calls=%async_computation.2 | async-start | bytes 524288 | tf_op jit(solution)/shard_map/all_to_all | solution.py:509
  110.8 29.8 %all-to-all-start.4 = ((bf16[8,128,512]{2,1,0:T(8,128)(2,1)}), bf16[8,128,512]{2,1,0:T(8,128)(2,1)S(1)}, u32[]{:S(2)}, u32[]{:S(2)}) async-start(bf16[8,128,512]{2,1,0:T(8,128)(2,1)} %get-tuple-element.69), calls=%async_computation.4 | async-start | bytes 2097152 | tf_op jit(solution)/shard_map/all_to_all | solution.py:509
  114.4 25.2 %collective-permute-start.2 = (bf16[4,128,512]{2,1,0:T(8,128)(2,1)}, bf16[4,128,512]{2,1,0:T(8,128)(2,1)S(1)}, u32[]{:S(2)}, u32[]{:S(2)}) collective-permute-start(bf16[4,128,512]{2,1,0:T(8,128)(2,1)} %get-tuple-element.71), channel_id=1, source_target_pairs={{0,1},{1,0},{2,3},{3,2},{4,5},{5,4},{6,7},{7,6},{8,9},{9,8},{10,11... | collective-permute-start | bytes 1572872 | tf_op jit(solution)/shard_map/ppermute | solution.py:505
  117.3 23.4 %copy-start.3 = (bf16[4,128,512]{2,1,0:T(8,128)(2,1)S(1)}, bf16[4,128,512]{2,1,0:T(8,128)(2,1)}, u32[]{:S(2)}) copy-start(bf16[4,128,512]{2,1,0:T(8,128)(2,1)} %get-tuple-element.62) | copy-start | bytes 1572868
  117.3 23.4 %copy-start.4 = (bf16[4,128,512]{2,1,0:T(8,128)(2,1)S(1)}, bf16[4,128,512]{2,1,0:T(8,128)(2,1)}, u32[]{:S(2)}) copy-start(bf16[4,128,512]{2,1,0:T(8,128)(2,1)} %get-tuple-element.73) | copy-start | bytes 1572868
  140.6 9.6 %copy-start.1 = (bf16[8,128,512]{2,1,0:T(8,128)(2,1)}, bf16[8,128,512]{2,1,0:T(8,128)(2,1)S(1)}, u32[]{:S(2)}) copy-start(bf16[8,128,512]{2,1,0:T(8,128)(2,1)S(1)} %all-to-all-done.4.e_ref) | copy-start | bytes 3145732
  141.7 27.0 %collective-permute-start.3 = (bf16[2,128,512]{2,1,0:T(8,128)(2,1)S(1)}, bf16[2,128,512]{2,1,0:T(8,128)(2,1)S(1)}, u32[]{:S(2)}, u32[]{:S(2)}) collective-permute-start(bf16[2,128,512]{2,1,0:T(8,128)(2,1)S(1)} %pad_maximum_fusion.1), channel_id=1, source_target_pairs={{0,2},{1,3},{2,0},{3,1},{4,6},{5,7},{6,4},{7,5},{8,10},{9,11},{10,... | collective-permute-start | bytes 786440 | tf_op jit(solution)/shard_map/ppermute | solution.py:505
  142.2 26.5 %collective-permute-start.4 = (bf16[2,128,512]{2,1,0:T(8,128)(2,1)S(1)}, bf16[2,128,512]{2,1,0:T(8,128)(2,1)S(1)}, u32[]{:S(2)}, u32[]{:S(2)}) collective-permute-start(bf16[2,128,512]{2,1,0:T(8,128)(2,1)S(1)} %pad_maximum_fusion.2), channel_id=1, source_target_pairs={{0,4},{1,5},{2,6},{3,7},{4,0},{5,1},{6,2},{7,3},{8,12},{9,13},{10,... | collective-permute-start | bytes 786440 | tf_op jit(solution)/shard_map/ppermute | solution.py:505
  144.6 24.1 %collective-permute-start.5 = (bf16[2,128,512]{2,1,0:T(8,128)(2,1)S(1)}, bf16[2,128,512]{2,1,0:T(8,128)(2,1)S(1)}, u32[]{:S(2)}, u32[]{:S(2)}) collective-permute-start(bf16[2,128,512]{2,1,0:T(8,128)(2,1)S(1)} %pad_maximum_fusion.3), channel_id=1, source_target_pairs={{0,6},{1,7},{2,4},{3,5},{4,2},{5,3},{6,0},{7,1},{8,14},{9,15},{10,... | collective-permute-start | bytes 786440 | tf_op jit(solution)/shard_map/ppermute | solution.py:505
  147.4 20.7 %all-to-all-start.5 = ((f32[32,1,4]{2,1,0:T(1,128)}), f32[32,1,4]{2,1,0:T(1,128)S(1)}, u32[]{:S(2)}, u32[]{:S(2)}) async-start(f32[32,1,4]{2,1,0:T(1,128)} %copy.23), calls=%async_computation.5 | async-start | bytes 32768 | tf_op jit(solution)/shard_map/all_to_all | solution.py:509
  168.7 0.7 copy-start.5
  168.7 0.8 copy-start.6
  168.7 0.9 copy-start.7

commit v3 on v2

--- a/solution.py
+++ b/solution.py
@@ -25,11 +25,10 @@
 BF = jnp.bfloat16
 F32 = jnp.float32
 HI = lax.Precision.HIGHEST
-VM = 56 * 1024 * 1024
-
-
-def params():
-    return pltpu.CompilerParams(vmem_limit_bytes=VM)
+
+
+def params(mib):
+    return pltpu.CompilerParams(vmem_limit_bytes=mib * 1024 * 1024)
 
 
 def dot(a, b):
@@ -146,7 +145,7 @@
             pltpu.VMEM((T, HEADS), F32),
             pltpu.VMEM((nrows, HEADS), F32),
         ],
-        compiler_params=params(),
+        compiler_params=params(56),
         name="prep",
     )(lengths, me, raw, bias, decay_log, gain)
 
@@ -191,8 +190,8 @@
         for src, halo, w_ref, bias, out, at, w in pieces:
             own = src[lo : lo + Q]
             window = jnp.concatenate([src[lo - 16 : lo] if j else halo[...], own], axis=0)
-            for c in range(0, w, 256):
-                c2 = min(c + 256, w)
+            for c in range(0, w, 512):
+                c2 = min(c + 512, w)
                 near3 = dot(pick[j], window[:, c:c2])
                 acc = bias[:, c:c2] + w_ref[KERNEL - 1 : KERNEL, c:c2] * own[:, c:c2].astype(F32)
                 for k in range(KERNEL - 1):
@@ -202,13 +201,13 @@
                 out[lo : lo + Q, c:c2] = y.astype(BF)
         scaled = act[lo : lo + Q, :GW] * dot(wst[lo : lo + Q], R)
         xhi, xlo = halves(scaled)
-        right = jnp.concatenate([xhi, xlo, xhi], axis=0)
+        right = jnp.concatenate([xhi, xlo], axis=0)
         bt = act[lo : lo + Q, GW : GW + STATE].T
         lane_seg = segment(lo + lax.broadcasted_iota(jnp.int32, (STATE, Q), 1), ends)
 
         def gathered(which, bt=bt, lane_seg=lane_seg, right=right):
-            bhi, blo = halves(jnp.where(lane_seg == which, bt, 0.0))
-            return dot(jnp.concatenate([bhi, bhi, blo], axis=1), right)
+            bhi = jnp.where(lane_seg == which, bt, 0.0).astype(BF)
+            return dot(jnp.concatenate([bhi, bhi], axis=1), right)
 
         if j:
             eloc[j - 1] = ent[...].astype(BF)
@@ -301,7 +300,7 @@
             pltpu.VMEM((SEQS, 16, GW), BF),
             pltpu.SemaphoreType.DMA((SEQS,)),
         ],
-        compiler_params=params(),
+        compiler_params=params(56),
         name="front",
     )(lengths, me, rows, rows, rows, halo, halo, halo, conv_weight, conv_weight, conv_weight, bias, bias, bias, wst, pick, small, gate)
 
@@ -357,7 +356,7 @@
         ],
         out_specs=pl.BlockSpec((T, GW), lambda g: (0, g)),
         out_shape=jax.ShapeDtypeStruct((T, INNER), F32),
-        compiler_params=params(),
+        compiler_params=params(56),
         cost_estimate=pl.CostEstimate(flops=8 * 10**9, bytes_accessed=2 * 10**7, transcendentals=5 * 10**6),
         name="local",
     )(lengths, me, xm, bm, cm, a2, b2, lead, eloc, small)
@@ -412,7 +411,7 @@
             sds((devices, 2 * SEQS, share), F32),
         ],
         scratch_shapes=[pltpu.VMEM((8, shard_w), F32), pltpu.VMEM((STATE, shard_w), F32)],
-        compiler_params=params(),
+        compiler_params=params(8),
         name="scan",
     )(lengths, me, got)
 
@@ -440,7 +439,7 @@
         in_specs=[SMEM, SMEM] + [VMEM] * (1 + len(pieces)),
         out_specs=VMEM,
         out_shape=jax.ShapeDtypeStruct((SEQS, shard_w, STATE), F32),
-        compiler_params=params(),
+        compiler_params=params(56),
         name="finals",
     )(lengths, me, base, *pieces)
 
@@ -471,20 +470,27 @@
         ],
         out_specs=pl.BlockSpec((tile, GW), lambda g, i: (i, g)),
         out_shape=jax.ShapeDtypeStruct((T, INNER), BF),
-        compiler_params=params(),
+        compiler_params=params(56),
         cost_estimate=pl.CostEstimate(flops=2 * 10**9, bytes_accessed=2 * 10**7, transcendentals=4 * 10**6),
         name="finish",
     )(y_local, gate, cm, enter, lead, norm)
 
 
-def largest_kernel(h_ref, w_ref, out):
+def largest_kernel(h_ref, w_ref, mail, out):
     logits = lax.dot_general(w_ref[...], h_ref[...], (((1,), (1,)), ((), ())), preferred_element_type=F32)
     top = jnp.max(logits, axis=0, keepdims=True)
     first = pl.program_id(0) == 0
     out[...] = jnp.where(first, top, jnp.maximum(top, out[...]))
 
-
-def largest(normed, vocab_weight):
+    @pl.when(pl.program_id(0) == pl.num_programs(0) - 1)
+    def _():
+        reqs = out.shape[1] // SEQS
+        seqs = mail.shape[0] // reqs
+        for b in range(reqs):
+            mail[b * seqs : (b + 1) * seqs] = jnp.broadcast_to(out[:, b * SEQS : (b + 1) * SEQS], (seqs, SEQS))
+
+
+def largest(normed, vocab_weight, devices):
     count, depth = normed.shape
     height = 1024
     return pl.pallas_call(
@@ -494,9 +500,10 @@
             pl.BlockSpec((count, depth), lambda i: (0, 0)),
             pl.BlockSpec((height, depth), lambda i: (i, 0)),
         ],
-        out_specs=pl.BlockSpec((1, count), lambda i: (0, 0)),
-        out_shape=jax.ShapeDtypeStruct((1, count), F32),
-        compiler_params=params(),
+        out_specs=pl.BlockSpec((devices, SEQS), lambda i: (0, 0)),
+        out_shape=jax.ShapeDtypeStruct((devices, SEQS), F32),
+        scratch_shapes=[pltpu.VMEM((1, count), F32)],
+        compiler_params=params(56),
         name="largest",
     )(normed, vocab_weight)
 
@@ -536,8 +543,7 @@
     rows_total = reqs * SEQS
     rows = conv_input[0]
 
-    edge = lax.ppermute(rows[T - (KERNEL - 1) :], "seq", [(i, i + 1) for i in range(seqs - 1)])
-    halo = jnp.pad(edge, ((16 - (KERNEL - 1), 0), (0, 0)))
+    halo = lax.ppermute(rows[T - 16 :], "seq", [(i, i + 1) for i in range(seqs - 1)])
     me = seq_place[None].astype(jnp.int32)
     lens = lengths[0].astype(jnp.int32)
     a2, b2, wst, leadj, lead0, pick, small = prep(
@@ -548,15 +554,23 @@
     )
     got = exchange(pay, "seq")
     y_local = local(lens, me, xm, bm, cm, a2, b2, leadj, eloc, small)
-    got, y_local = lax.optimization_barrier((got, y_local))
+    given = [swap(slots[2], seqs, 1)]
+    got, y_local, given = lax.optimization_barrier((got, y_local, given))
     enter, base, mail = scan(lens, me, T, got, devices, share)
 
     mail, slots = lax.optimization_barrier((mail, slots))
-    given = [swap(slots[2], seqs, 1)]
+    given.append(swap(slots[3], seqs, 1))
     mail = exchange(mail, every)
-    mail, given, kept = lax.optimization_barrier((mail, given, slots[3]))
-    given.append(swap(kept, seqs, 1))
+    mail, given = lax.optimization_barrier((mail, given))
     mail = mail.reshape(reqs, seqs, 2 * SEQS, share)
+    pair = seq_place // 2
+
+    def tail(c):
+        return jnp.stack([
+            lax.dynamic_index_in_dim(kept, pair ^ c, 0, keepdims=False) + lax.dynamic_index_in_dim(other, pair ^ c, 0, keepdims=False)
+            for kept, other in zip(slots[:2], given)
+        ])
+
     v = lax.dynamic_index_in_dim(mail[:, :, :SEQS], flat * share // shard_w, 1, keepdims=False)
     near = GW // shard_w
     squares = lax.dynamic_slice_in_dim(mail[:, :, SEQS:], flat * share // GW * near, near, 1).sum(axis=1)
@@ -564,31 +578,28 @@
     u = (v * lax.dynamic_slice_in_dim(norm_weight, flat * share, share)).astype(BF).reshape(rows_total, share)
     partial = jnp.dot(u, out_weight, preferred_element_type=F32)
     chunk = D // devices
+    early = [seqs // 4]
+    tails = {c: swap(tail(c), seqs, 2 * c) for c in early}
     mail = exchange(partial.reshape(rows_total, devices, chunk).transpose(1, 0, 2), every)
+    mail, tails = lax.optimization_barrier((mail, tails))
     own = mail.sum(axis=0)
     residual = residual_last.reshape(rows_total, D)
     own = own + lax.dynamic_slice_in_dim(residual, flat * chunk, chunk, 1).astype(F32)
     mail = exchange(jnp.broadcast_to(own.astype(BF), (devices, rows_total, chunk)), every).astype(F32)
     hidden = mail.transpose(1, 0, 2).reshape(rows_total, D)
-    hidden, enter = lax.optimization_barrier((hidden, enter))
+    hidden, enter, tails = lax.optimization_barrier((hidden, enter, tails))
     entering = exchange(enter, "seq")
     rms = lax.rsqrt(jnp.mean(hidden * hidden, axis=-1, keepdims=True) + TINY_FLOOR)
     normed = (hidden * rms * final_gain).astype(BF)
     last_hidden = lax.dynamic_slice_in_dim(hidden.reshape(reqs, SEQS, D), req_place, 1, 0).astype(BF)
-    top = largest(normed, vocab_weight).reshape(reqs, 1, SEQS)
-    top = jnp.broadcast_to(top, (reqs, seqs, SEQS)).reshape(devices, SEQS)
-    top, entering, given = lax.optimization_barrier((top, entering, given))
-
-    pair = seq_place // 2
-    tails = [
-        jnp.stack([
-            lax.dynamic_index_in_dim(kept, pair ^ c, 0, keepdims=False) + lax.dynamic_index_in_dim(other, pair ^ c, 0, keepdims=False)
-            for kept, other in zip(slots[:2], given)
-        ])
-        for c in range(seqs // 2)
-    ]
-    tails, entering = lax.optimization_barrier((tails, entering))
-    tails = [tails[0]] + [swap(tails[c], seqs, 2 * c) for c in range(1, seqs // 2)]
+    top = largest(normed, vocab_weight, devices)
+    top, entering = lax.optimization_barrier((top, entering))
+
+    late = [c for c in range(seqs // 2) if c not in early]
+    rest, entering = lax.optimization_barrier(([tail(c) for c in late], entering))
+    for c, x in zip(late, rest):
+        tails[c] = swap(x, seqs, 2 * c) if c else x
+    tails = [tails[c] for c in range(seqs // 2)]
     y_gated = finish(y_local, gate_projected[0], cm, entering, lead0, norm_weight[None])
 
     max_logit = jnp.max(exchange(top, every), axis=0, keepdims=True)

time: 174 us -> 171 us (0.983)
  Pallas kernels: 67.4 us -> 65 us
    ppermute x5, waiting for transfers between devices: 5.56 us -> 28.7 us  [swap(): return lax.ppermute(x, 'seq', [(i, i ^ distance) for i in range(seqs)])]
    all_to_all x5, waiting for transfers between devices: 42.3 us -> 20.5 us  [exchange(): return lax.all_to_all(x, axes, 0, 0, tiled=True)]
    all_to_all x5, starting transfers between devices: 22.1 us -> 20.3 us  [exchange(): return lax.all_to_all(x, axes, 0, 0, tiled=True)]
  transfers between devices with their start and end apart: 11 -> 11, of which waited for: 6 -> 5; matrix products, arithmetic and copies ran while one was open for 4% -> 3% of each run, Pallas kernels for 23% -> 23%
where the time goes in v3:
time: 171 us; the launch traced here: 170 us
  Pallas kernels  65 us (38%)
  waiting for transfers between devices  49.1 us (29%)
  starting transfers between devices  33.2 us (19%)
  blocking collectives  11.2 us (7%)
  local copies, waits for them, and re-layouts  5.66 us (3%)
  other arithmetic  3.77 us (2%)
    ppermute x5, waiting for transfers between devices, swap(): return lax.ppermute(x, 'seq', [(i, i ^ distance) for i in range(seqs)])  28.7 us
    all_to_all x5, waiting for transfers between devices, exchange(): return lax.all_to_all(x, axes, 0, 0, tiled=True)  20.5 us
    all_to_all x5, starting transfers between devices, exchange(): return lax.all_to_all(x, axes, 0, 0, tiled=True)  20.3 us
    pallas_call x1, Pallas kernels, front(): pl.pallas_call(functools.partial(front_kernel, seqs, shard_w), grid=(GROU...  17.9 us
    pallas_call x1, Pallas kernels, largest(): pl.pallas_call(largest_kernel, grid=(vocab_weight.shape[0] // height,), i...  14.7 us
    all_to_all x1, blocking collectives, exchange(): return lax.all_to_all(x, axes, 0, 0, tiled=True)  11.2 us
    pallas_call x1, Pallas kernels, local(): pl.pallas_call(functools.partial(local_kernel, n + 2 * SEQS + 1), grid=(G...  11.1 us
    pallas_call x1, Pallas kernels, finish(): pl.pallas_call(finish_kernel, grid=(GROUPS, T // tile), in_specs=[pl.Bloc...  10.5 us
  transfers between devices with their start and end apart: 11, of which 5 were waited for; matrix products, arithmetic and copies ran while one was open for 3% of the time, Pallas kernels for 23%

profile of v3, /device:TPU:0, one launch (start us, length us, event | category | flops | bytes accessed | tf_op | source)
XLA Modules:
  0.0 170.0 jit_solution(2853779023898925120)
XLA Ops:
  0.6 0.9 slice_bitcast_fusion
  1.6 4.9 %collective-permute-start = (bf16[16,5120]{1,0:T(8,128)(2,1)S(1)}, bf16[16,5120]{1,0:T(8,128)(2,1)S(1)}, u32[]{:S(2)}, u32[]{:S(2)}) collective-permute-start(bf16[16,5120]{1,0:T(8,128)(2,1)S(1)} %slice_bitcast_fusion), channel_id=1, source_target_pairs={{0,1},{1,2},{2,3},{3,4},{4,5},{5,6},{6,7},{8,9},{9,10},{10,11},{11... | collective-permute-start | bytes 491528 | tf_op jit(solution)/shard_map/ppermute | solution.py:546
  6.5 3.5 %prep.1 = (f32[4,512,16]{2,1,0:T(8,128)}, f32[64,512]{1,0:T(8,128)}, bf16[512,128]{1,0:T(8,128)(2,1)}, bf16[512,128]{1,0:T(8,128)(2,1)}, bf16[512,128]{1,0:T(8,1...) custom-call(s32[4]{0:T(128)} %bitcast.42, s32[1]{0:T(128)} %bitcast.1.me, f32[64,512]{1,0:T(8,128)} %bitcast.60, ...), custom_call_target="tpu_custom_call" | custom-call | tf_op jit(solution)/shard_map/prep/pallas_call | solution.py:129
  10.0 0.0 collective-permute-done.hx.hb.hc
  10.0 0.0 copy-start.3
  10.0 0.7 copy-done.3
  10.6 17.9 %front.1 = (bf16[512,4096]{1,0:T(8,128)(2,1)}, bf16[512,512]{1,0:T(8,128)(2,1)}, bf16[512,512]{1,0:T(8,128)(2,1)}, bf16[8,144,512]{2,1,0:T(8,128)(2,1)}, bf16[3,...) custom-call(s32[4]{0:T(128)} %bitcast.43, ...), custom_call_target="tpu_custom_call" | custom-call | tf_op jit(solution)/shard_map/front/pallas_call | solution.py:271
  28.6 6.5 %all-to-all-start = ((bf16[8,144,512]{2,1,0:T(8,128)(2,1)}), bf16[8,144,512]{2,1,0:T(8,128)(2,1)S(1)}, u32[]{:S(2)}, u32[]{:S(2)}) async-start(bf16[8,144,512]{2,1,0:T(8,128)(2,1)} %get-tuple-element.47), calls=%async_computation | async-start | bytes 2359296 | tf_op jit(solution)/shard_map/all_to_all | solution.py:516
  35.1 2.0 %collective-permute-start.1 = (bf16[4,128,512]{2,1,0:T(8,128)(2,1)}, bf16[4,128,512]{2,1,0:T(8,128)(2,1)}, u32[]{:S(2)}, u32[]{:S(2)}) collective-permute-start(bf16[4,128,512]{2,1,0:T(8,128)(2,1)} %get-tuple-element.55), channel_id=1, source_target_pairs={{0,1},{1,0},{2,3},{3,2},{4,5},{5,4},{6,7},{7,6},{8,9},{9,8},{10,11... | collective-permute-start | bytes 1572872 | tf_op jit(solution)/shard_map/ppermute | solution.py:512
  37.1 0.0 copy-start.1
  37.1 0.0 copy-start.4
  37.1 11.1 %local.1.y_ref = f32[512,4096]{1,0:T(8,128)} custom-call(s32[4]{0:T(128)} %bitcast.44, s32[1]{0:T(128)} %bitcast.1.me, bf16[512,4096]{1,0:T(8,128)(2,1)} %get-tuple-element.48.x_ref, bf16[512,512]{1,0:T(8,128)(2,1)} %get-tuple-element.49.b_ref, bf16[512,512]{1,0:T(8,128)(2,1)} %get-tuple-element.50.c_ref, f32[4,512,16]{2,1,0:T(8,128)} %get-tuple-element.51.a_ref, ...), custom_call_target="tpu_custom_call" | custom-call | flops 8000000000 | bytes 20000000 | tf_op jit(solution)/shard_map/local/pallas_call | solution.py:342
  48.2 0.0 copy-start.5
  48.2 0.0 copy-start.6
  48.2 12.3 %collective-permute-done.1 = bf16[4,128,512]{2,1,0:T(8,128)(2,1)} collective-permute-done((bf16[4,128,512]{2,1,0:T(8,128)(2,1)}, bf16[4,128,512]{2,1,0:T(8,128)(2,1)}, u32[]{:S(2)}, u32[]{:S(2)}) %collective-permute-start.1) | collective-permute-done | bytes 524320 | tf_op jit(solution)/shard_map/ppermute | solution.py:512
  60.5 2.5 %all-to-all-done.got = bf16[8,144,512]{2,1,0:T(8,128)(2,1)S(1)} async-done(((bf16[8,144,512]{2,1,0:T(8,128)(2,1)}), bf16[8,144,512]{2,1,0:T(8,128)(2,1)S(1)}, u32[]{:S(2)}, u32[]{:S(2)}) %all-to-all-start) | async-done | bytes 1179680 | tf_op jit(solution)/shard_map/all_to_all | solution.py:516
  63.0 0.0 copy-done.1
  63.0 3.9 %scan.1 = (bf16[8,128,512]{2,1,0:T(8,128)(2,1)}, f32[4,128,512]{2,1,0:T(8,128)S(1)}, f32[32,8,128]{2,1,0:T(8,128)}) custom-call(s32[4]{0:T(128)S(1)} %bitcast.46, s32[1]{0:T(128)} %bitcast.1.me, bf16[8,144,512]{2,1,0:T(8,128)(2,1)S(1)} %all-to-all-done.got), custom_call_target="tpu_custom_call" | custom-call | tf_op jit(solution)/shard_map/scan/pallas_call | solution.py:404
  66.9 0.0 copy-start
  66.9 1.1 copy-done
  67.9 0.0 copy-start.10
  67.9 1.2 collective-permute-start.2
  69.2 3.0 %all-to-all-start.1 = ((f32[32,8,128]{2,1,0:T(8,128)}), f32[32,8,128]{2,1,0:T(8,128)S(1)}, u32[]{:S(2)}, u32[]{:S(2)}) async-start(f32[32,8,128]{2,1,0:T(8,128)} %get-tuple-element.63), calls=%async_computation.1 | async-start | bytes 262144 | tf_op jit(solution)/shard_map/all_to_all | solution.py:516
  72.2 0.0 copy-done.4
  72.2 0.7 copy.24
  72.9 0.8 dynamic_slice.79
  73.7 8.2 %all-to-all-done.1 = f32[32,8,128]{2,1,0:T(8,128)S(1)} async-done(((f32[32,8,128]{2,1,0:T(8,128)}), f32[32,8,128]{2,1,0:T(8,128)S(1)}, u32[]{:S(2)}, u32[]{:S(2)}) %all-to-all-start.1) | async-done | bytes 131104 | tf_op jit(solution)/shard_map/all_to_all | solution.py:516
  81.9 0.0 collective-permute-done.2
  82.0 1.1 convolution_bitcast_fusion
  83.1 4.2 %all-to-all-start.2 = ((f32[32,16,128]{2,1,0:T(8,128)}), f32[32,16,128]{2,1,0:T(8,128)S(1)}, u32[]{:S(2)}, u32[]{:S(2)}) async-start(f32[32,16,128]{2,1,0:T(8,128)} %convolution_bitcast_fusion), calls=%async_computation.2 | async-start | bytes 524288 | tf_op jit(solution)/shard_map/all_to_all | solution.py:516
  87.3 0.0 copy-done.5
  87.3 0.0 copy-done.6
  87.3 0.0 copy-start.11
  87.3 1.4 dynamic-slice_add_fusion
  88.8 2.7 %collective-permute-start.3 = (bf16[2,128,512]{2,1,0:T(8,128)(2,1)S(1)}, bf16[2,128,512]{2,1,0:T(8,128)(2,1)S(1)}, u32[]{:S(2)}, u32[]{:S(2)}) collective-permute-start(bf16[2,128,512]{2,1,0:T(8,128)(2,1)S(1)} %pad_maximum_fusion.3), channel_id=1, source_target_pairs={{0,4},{1,5},{2,6},{3,7},{4,0},{5,1},{6,2},{7,3},{8,12},{9,13},{10,... | collective-permute-start | bytes 786440 | tf_op jit(solution)/shard_map/ppermute | solution.py:512
  91.5 0.0 copy-done.10
  91.5 16.4 %collective-permute-done.3.refs_2_ = bf16[2,128,512]{2,1,0:T(8,128)(2,1)S(1)} collective-permute-done((bf16[2,128,512]{2,1,0:T(8,128)(2,1)S(1)}, bf16[2,128,512]{2,1,0:T(8,128)(2,1)S(1)}, u32[]{:S(2)}, u32[]{:S(2)}) %collective-permute-start.3) | collective-permute-done | bytes 262176 | tf_op jit(solution)/shard_map/ppermute | solution.py:512
  107.9 0.0 copy-start.7
  107.9 0.0 all-to-all-done.2
  108.0 11.2 %all_to_all.34 = bf16[32,16,128]{2,1,0:T(8,128)(2,1)S(1)} all-to-all(bf16[32,16,128]{2,1,0:T(8,128)(2,1)S(1)} %broadcast_in_dim.35), channel_id=1, replica_groups=mesh['req'=4,'seq'=8] {'req','seq'}, dimensions={0} | all-to-all | bytes 262144 | tf_op jit(solution)/shard_map/all_to_all | solution.py:516
  119.2 3.6 %all-to-all-start.4 = ((bf16[8,128,512]{2,1,0:T(8,128)(2,1)}), bf16[8,128,512]{2,1,0:T(8,128)(2,1)S(1)}, u32[]{:S(2)}, u32[]{:S(2)}) async-start(bf16[8,128,512]{2,1,0:T(8,128)(2,1)} %get-tuple-element.74), calls=%async_computation.4 | async-start | bytes 2097152 | tf_op jit(solution)/shard_map/all_to_all | solution.py:516
  122.8 0.7 pad_maximum_fusion.refs_0_
  123.5 0.1 reshape.73
  123.6 0.1 multiply_reduce_fusion
  123.8 0.0 copy-done.11
  123.8 0.8 multiply_convert_fusion.h_ref
  124.5 14.7 %largest.1 = f32[32,4]{1,0:T(8,128)} custom-call(bf16[16,4096]{1,0:T(8,128)(2,1)} %multiply_convert_fusion.h_ref, bf16[4096,4096]{1,0:T(8,128)(2,1)} %w_ref.1), custom_call_target="tpu_custom_call" | custom-call | tf_op jit(solution)/shard_map/largest/pallas_call | solution.py:496
  139.3 0.0 copy-done.7
  139.3 9.7 %all-to-all-done.4.e_ref = bf16[8,128,512]{2,1,0:T(8,128)(2,1)S(1)} async-done(((bf16[8,128,512]{2,1,0:T(8,128)(2,1)}), bf16[8,128,512]{2,1,0:T(8,128)(2,1)S(1)}, u32[]{:S(2)}, u32[]{:S(2)}) %all-to-all-start.4) | async-done | bytes 1048608 | tf_op jit(solution)/shard_map/all_to_all | solution.py:516
  149.0 0.0 copy-start.2
  149.0 0.0 collective-permute-start.4
  149.0 2.1 %collective-permute-start.5 = (bf16[2,128,512]{2,1,0:T(8,128)(2,1)S(1)}, bf16[2,128,512]{2,1,0:T(8,128)(2,1)S(1)}, u32[]{:S(2)}, u32[]{:S(2)}) collective-permute-start(bf16[2,128,512]{2,1,0:T(8,128)(2,1)S(1)} %pad_maximum_fusion.2), channel_id=1, source_target_pairs={{0,6},{1,7},{2,4},{3,5},{4,2},{5,3},{6,0},{7,1},{8,14},{9,15},{10,... | collective-permute-start | bytes 786440 | tf_op jit(solution)/shard_map/ppermute | solution.py:512
  151.1 0.6 dynamic-slice_convert_fusion
  151.7 3.1 %all-to-all-start.5 = ((f32[32,1,4]{2,1,0:T(1,128)}), f32[32,1,4]{2,1,0:T(1,128)S(1)}, u32[]{:S(2)}, u32[]{:S(2)}) async-start(f32[32,1,4]{2,1,0:T(1,128)} %bitcast.61), calls=%async_computation.5 | async-start | bytes 32768 | tf_op jit(solution)/shard_map/all_to_all | solution.py:516
  154.8 0.0 copy-done.2
  154.8 10.5 %finish.1 = bf16[512,4096]{1,0:T(8,128)(2,1)} custom-call(f32[512,4096]{1,0:T(8,128)} %local.1.y_ref, bf16[512,4096]{1,0:T(8,128)(2,1)} %bitcast.51, bf16[512,512]{1,0:T(8,128)(2,1)} %get-tuple-element.50.c_ref, bf16[8,128,512]{2,1,0:T(8,128)(2,1)} %copy-done.2, bf16[512,128]{1,0:T(8,128)(2,1)} %get-tuple-element.77.lead, f32[1,4096]{1,0:T(1,128)} %bitcast.63), custom_call_target="tpu_custom_call" | custom-call | flops 2000000000 | bytes 20000000 | tf_op jit(solution)/shard_map/finish/pallas_call | solution.py:460
  165.3 0.0 all-to-all-done.5
  165.3 0.6 reduce_max.9
  165.8 0.0 collective-permute-done.4.refs_1_
  165.8 0.0 copy-start.8
  165.8 0.0 collective-permute-done.5.refs_3_
  165.8 0.7 copy-done.8
  166.5 0.1 copy-done.9
  166.6 3.3 %finals.1 = f32[4,512,128]{2,1,0:T(8,128)} custom-call(s32[4]{0:T(128)} %bitcast.45, s32[1]{0:T(128)} %bitcast.1.me, f32[4,128,512]{2,1,0:T(8,128)} %copy-done, bf16[2,128,512]{2,1,0:T(8,128)(2,1)} %pad_maximum_fusion.refs_0_, bf16[2,128,512]{2,1,0:T(8,128)(2,1)} %copy-done.8, bf16[2,128,512]{2,1,0:T(8,128)(2,1)} %copy-done.7, bf16[2,128,512]{2,1,0:T(8,128)(2,1)} %copy-done.9), custom_call_target="tpu_custom_call" | custom-call | tf_op jit(solution)/shard_map/finals/pallas_call | solution.py:437
  (13 shorter events, 0.3 us)
Async XLA Ops:
  1.6 8.4 %collective-permute-start = (bf16[16,5120]{1,0:T(8,128)(2,1)S(1)}, bf16[16,5120]{1,0:T(8,128)(2,1)S(1)}, u32[]{:S(2)}, u32[]{:S(2)}) collective-permute-start(bf16[16,5120]{1,0:T(8,128)(2,1)S(1)} %slice_bitcast_fusion), channel_id=1, source_target_pairs={{0,1},{1,2},{2,3},{3,4},{4,5},{5,6},{6,7},{8,9},{9,10},{10,11},{11... | collective-permute-start | bytes 491528 | tf_op jit(solution)/shard_map/ppermute | solution.py:546
  10.0 0.7 copy-start.3
  28.6 34.4 %all-to-all-start = ((bf16[8,144,512]{2,1,0:T(8,128)(2,1)}), bf16[8,144,512]{2,1,0:T(8,128)(2,1)S(1)}, u32[]{:S(2)}, u32[]{:S(2)}) async-start(bf16[8,144,512]{2,1,0:T(8,128)(2,1)} %get-tuple-element.47), calls=%async_computation | async-start | bytes 2359296 | tf_op jit(solution)/shard_map/all_to_all | solution.py:516
  35.1 25.5 %collective-permute-start.1 = (bf16[4,128,512]{2,1,0:T(8,128)(2,1)}, bf16[4,128,512]{2,1,0:T(8,128)(2,1)}, u32[]{:S(2)}, u32[]{:S(2)}) collective-permute-start(bf16[4,128,512]{2,1,0:T(8,128)(2,1)} %get-tuple-element.55), channel_id=1, source_target_pairs={{0,1},{1,0},{2,3},{3,2},{4,5},{5,4},{6,7},{7,6},{8,9},{9,8},{10,11... | collective-permute-start | bytes 1572872 | tf_op jit(solution)/shard_map/ppermute | solution.py:512
  37.1 25.9 %copy-start.1 = (s32[1,4]{1,0:T(1,128)S(1)}, s32[1,4]{1,0:T(1,128)}, u32[]{:S(2)}) copy-start(s32[1,4]{1,0:T(1,128)} %param.23) | copy-start | bytes 52
  37.1 35.1 %copy-start.4 = (bf16[128,4096]{1,0:T(8,128)(2,1)S(1)}, bf16[128,4096]{1,0:T(8,128)(2,1)}, u32[]{:S(2)}) copy-start(bf16[128,4096]{1,0:T(8,128)(2,1)} %param.24) | copy-start | bytes 3145732
  48.2 39.1 %copy-start.5 = (bf16[4,128,512]{2,1,0:T(8,128)(2,1)S(1)}, bf16[4,128,512]{2,1,0:T(8,128)(2,1)}, u32[]{:S(2)}) copy-start(bf16[4,128,512]{2,1,0:T(8,128)(2,1)} %get-tuple-element.62) | copy-start | bytes 1572868
  48.2 39.1 %copy-start.6 = (bf16[4,128,512]{2,1,0:T(8,128)(2,1)S(1)}, bf16[4,128,512]{2,1,0:T(8,128)(2,1)}, u32[]{:S(2)}) copy-start(bf16[4,128,512]{2,1,0:T(8,128)(2,1)} %get-tuple-element.67) | copy-start | bytes 1572868
  66.9 1.1 copy-start
  67.9 23.6 %copy-start.10 = (bf16[4,4,4096]{2,1,0:T(4,128)(2,1)S(1)}, bf16[4,4,4096]{2,1,0:T(4,128)(2,1)}, u32[]{:S(2)}) copy-start(bf16[4,4,4096]{2,1,0:T(4,128)(2,1)} %param.25) | copy-start | bytes 393220
  67.9 14.0 %collective-permute-start.2 = (bf16[4,128,512]{2,1,0:T(8,128)(2,1)}, bf16[4,128,512]{2,1,0:T(8,128)(2,1)}, u32[]{:S(2)}, u32[]{:S(2)}) collective-permute-start(bf16[4,128,512]{2,1,0:T(8,128)(2,1)} %get-tuple-element.65), channel_id=1, source_target_pairs={{0,1},{1,0},{2,3},{3,2},{4,5},{5,4},{6,7},{7,6},{8,9},{9,8},{10,11... | collective-permute-start | bytes 1572872 | tf_op jit(solution)/shard_map/ppermute | solution.py:512
  69.2 12.8 %all-to-all-start.1 = ((f32[32,8,128]{2,1,0:T(8,128)}), f32[32,8,128]{2,1,0:T(8,128)S(1)}, u32[]{:S(2)}, u32[]{:S(2)}) async-start(f32[32,8,128]{2,1,0:T(8,128)} %get-tuple-element.63), calls=%async_computation.1 | async-start | bytes 262144 | tf_op jit(solution)/shard_map/all_to_all | solution.py:516
  83.1 24.8 %all-to-all-start.2 = ((f32[32,16,128]{2,1,0:T(8,128)}), f32[32,16,128]{2,1,0:T(8,128)S(1)}, u32[]{:S(2)}, u32[]{:S(2)}) async-start(f32[32,16,128]{2,1,0:T(8,128)} %convolution_bitcast_fusion), calls=%async_computation.2 | async-start | bytes 524288 | tf_op jit(solution)/shard_map/all_to_all | solution.py:516
  87.3 36.5 %copy-start.11 = (f32[4096]{0:T(1024)S(1)}, f32[4096]{0:T(1024)}, u32[]{:S(2)}) copy-start(f32[4096]{0:T(1024)} %param.26) | copy-start | bytes 49156
  88.8 19.1 %collective-permute-start.3 = (bf16[2,128,512]{2,1,0:T(8,128)(2,1)S(1)}, bf16[2,128,512]{2,1,0:T(8,128)(2,1)S(1)}, u32[]{:S(2)}, u32[]{:S(2)}) collective-permute-start(bf16[2,128,512]{2,1,0:T(8,128)(2,1)S(1)} %pad_maximum_fusion.3), channel_id=1, source_target_pairs={{0,4},{1,5},{2,6},{3,7},{4,0},{5,1},{6,2},{7,3},{8,12},{9,13},{10,... | collective-permute-start | bytes 786440 | tf_op jit(solution)/shard_map/ppermute | solution.py:512
  107.9 31.4 %copy-start.7 = (bf16[2,128,512]{2,1,0:T(8,128)(2,1)}, bf16[2,128,512]{2,1,0:T(8,128)(2,1)S(1)}, u32[]{:S(2)}) copy-start(bf16[2,128,512]{2,1,0:T(8,128)(2,1)S(1)} %collective-permute-done.3.refs_2_) | copy-start | bytes 786436
  119.2 29.8 %all-to-all-start.4 = ((bf16[8,128,512]{2,1,0:T(8,128)(2,1)}), bf16[8,128,512]{2,1,0:T(8,128)(2,1)S(1)}, u32[]{:S(2)}, u32[]{:S(2)}) async-start(bf16[8,128,512]{2,1,0:T(8,128)(2,1)} %get-tuple-element.74), calls=%async_computation.4 | async-start | bytes 2097152 | tf_op jit(solution)/shard_map/all_to_all | solution.py:516
  149.0 5.8 %copy-start.2 = (bf16[8,128,512]{2,1,0:T(8,128)(2,1)}, bf16[8,128,512]{2,1,0:T(8,128)(2,1)S(1)}, u32[]{:S(2)}) copy-start(bf16[8,128,512]{2,1,0:T(8,128)(2,1)S(1)} %all-to-all-done.4.e_ref) | copy-start | bytes 3145732
  149.0 16.8 %collective-permute-start.4 = (bf16[2,128,512]{2,1,0:T(8,128)(2,1)S(1)}, bf16[2,128,512]{2,1,0:T(8,128)(2,1)S(1)}, u32[]{:S(2)}, u32[]{:S(2)}) collective-permute-start(bf16[2,128,512]{2,1,0:T(8,128)(2,1)S(1)} %pad_maximum_fusion.1), channel_id=1, source_target_pairs={{0,2},{1,3},{2,0},{3,1},{4,6},{5,7},{6,4},{7,5},{8,10},{9,11},{10,... | collective-permute-start | bytes 786440 | tf_op jit(solution)/shard_map/ppermute | solution.py:512
  149.0 16.8 %collective-permute-start.5 = (bf16[2,128,512]{2,1,0:T(8,128)(2,1)S(1)}, bf16[2,128,512]{2,1,0:T(8,128)(2,1)S(1)}, u32[]{:S(2)}, u32[]{:S(2)}) collective-permute-start(bf16[2,128,512]{2,1,0:T(8,128)(2,1)S(1)} %pad_maximum_fusion.2), channel_id=1, source_target_pairs={{0,6},{1,7},{2,4},{3,5},{4,2},{5,3},{6,0},{7,1},{8,14},{9,15},{10,... | collective-permute-start | bytes 786440 | tf_op jit(solution)/shard_map/ppermute | solution.py:512
  151.7 13.6 %all-to-all-start.5 = ((f32[32,1,4]{2,1,0:T(1,128)}), f32[32,1,4]{2,1,0:T(1,128)S(1)}, u32[]{:S(2)}, u32[]{:S(2)}) async-start(f32[32,1,4]{2,1,0:T(1,128)} %bitcast.61), calls=%async_computation.5 | async-start | bytes 32768 | tf_op jit(solution)/shard_map/all_to_all | solution.py:516
  165.8 0.7 copy-start.8
  165.8 0.8 copy-start.9
